TPU v7x, 32 devices: a whole 2x2x4 slice. The times are simulated.
32 devices in a mesh: layer: 8 (over z, x), ctx: 4 (over y, core).
Axes of the slice: x: 2, y: 2, z: 4, core: 2. Of those that a mesh axis runs over, the one named last changes fastest.
Arguments:
- queries: bfloat16 [8, 512, 1536], P('layer', 'ctx'), may hold values from -9 to 9
- keys: bfloat16 [512, 512], P(('ctx', 'layer')), may hold values from -4 to 4
- values: bfloat16 [512, 512], P(('ctx', 'layer')), may hold values from -6 to 6
- head: float32 [8, 1536, 2], P('layer'), may hold values from -1.5 to 1.5
- segments: int32 [512], replicated, may hold values from 0 to 4, as said below
- label_mask: int32 [512], P('ctx'), may hold values 0 or 1
- labels: int32 [512], P('ctx'), may hold values from 0 to 1
Outputs:
- loss: float32 [8], P('layer')
- query_gradient: float32 [8, 512, 1536], P('layer', 'ctx')
- grad_keys: float32 [512, 512], P(('ctx', 'layer'))
- grad_values: float32 [512, 512], P(('ctx', 'layer'))
- head_gradient_rows: float32 [8, 1536, 2], P('layer')
Inputs may be any that keep to these rules, and one draw needn't show every extreme that they name: `segments`: document ids never fall; the first document spans exactly 384 positions and the positions after it form exactly four more documents, each of one position or more.
All inputs are finite; a program needn't handle non-finite values. No bound on the sum of `label_mask` on one device may be relied on, other than what follows from the above.
Results may differ from a plain program's by a relative error of at most 0.019.
Values may be sent and summed in bfloat16 or wider, within the bound.
A program may use at most 128 MiB of HBM per device.

v0:
```python
import jax
import jax.numpy as jnp
from jax import lax
from jax.sharding import PartitionSpec as P

QUERY_HEADS = 12
KEY_VALUE_HEADS = 4
HEAD_WIDTH = 128
CLASSES = 2


NEGATIVE_FILL = -1e30
HIGH = lax.Precision.HIGHEST


def masked_scores(query_tensor_four, key_block, seg_q, seg_k, q_start, k_start):
    row_count = key_block.shape[0]
    key_tensor_three = key_block.reshape(row_count, KEY_VALUE_HEADS, HEAD_WIDTH)
    s = jnp.einsum(
        "tgrd,ngd->tgrn", query_tensor_four, key_tensor_three, preferred_element_type=jnp.float32
    ) * HEAD_WIDTH ** (-0.5)
    q_pos = q_start + jnp.arange(query_tensor_four.shape[0], dtype=jnp.int32)
    k_pos = k_start + jnp.arange(row_count, dtype=jnp.int32)
    allowed = (k_pos[None, :] <= q_pos[:, None]) & (seg_k[None, :] == seg_q[:, None])
    return jnp.where(allowed[:, None, None, :], s, NEGATIVE_FILL)


def per_device(queries, keys, values, head, segments, label_mask, labels):
    local_tokens = queries.shape[1]
    n_ctx = lax.axis_size("ctx")
    ctx_index = lax.axis_index("ctx")
    own_start = ctx_index * local_tokens
    own_last = own_start + local_tokens - 1
    head_group = QUERY_HEADS // KEY_VALUE_HEADS
    query_tensor_four = queries[0].reshape(local_tokens, KEY_VALUE_HEADS, head_group, HEAD_WIDTH)
    seg_q = lax.dynamic_slice_in_dim(segments, own_start, local_tokens)
    head_layer = head[0]

    def reaches(k_start, row_count):
        last = jnp.minimum(k_start + row_count, own_start + local_tokens) - 1
        return (k_start <= own_last) & (segments[jnp.maximum(last, 0)] >= segments[own_start])

    key_whole, value_whole = (
        lax.all_gather(keys, "layer", axis=0, tiled=True),
        lax.all_gather(values, "layer", axis=0, tiled=True),
    )
    begin = (
        jnp.full((local_tokens, KEY_VALUE_HEADS, head_group), NEGATIVE_FILL, jnp.float32),
        jnp.zeros((local_tokens, KEY_VALUE_HEADS, head_group), jnp.float32),
        jnp.zeros((local_tokens, KEY_VALUE_HEADS, head_group, HEAD_WIDTH), jnp.float32),
    )
    start_offset = jnp.int32(0)
    k_piece = lax.all_gather(key_whole, "ctx", axis=0, tiled=True)
    value_portion = lax.all_gather(value_whole, "ctx", axis=0, tiled=True)
    row_count = k_piece.shape[0]

    def update(inner):
        top, total, acc = inner
        s = masked_scores(query_tensor_four, k_piece, seg_q, segments, own_start, start_offset)
        new_top = jnp.maximum(top, jnp.max(s, axis=-1))
        weights = jnp.exp(s - new_top[..., None])
        value_tensor_three = value_portion.reshape(row_count, KEY_VALUE_HEADS, HEAD_WIDTH).astype(
            jnp.float32
        )
        acc = jnp.einsum("tgrn,ngd->tgrd", weights, value_tensor_three, precision=HIGH)
        return (new_top, jnp.sum(weights, axis=-1), acc)

    top, total, acc = lax.cond(reaches(start_offset, row_count), update, lambda inner: inner, begin)
    lse = top + jnp.log(total)
    flat_rows = (acc / total[..., None]).reshape(local_tokens, QUERY_HEADS * HEAD_WIDTH)
    logits = jnp.dot(flat_rows, head_layer, precision=HIGH)
    biggest = jnp.max(logits, axis=-1)
    log_total = biggest + jnp.log(jnp.sum(jnp.exp(logits - biggest[:, None]), axis=-1))
    onehot = (labels[:, None] == jnp.arange(CLASSES, dtype=jnp.int32)[None, :]).astype(jnp.float32)
    mask = label_mask.astype(jnp.float32)
    loss_part = jnp.sum(mask * (log_total - jnp.sum(onehot * logits, axis=-1)))
    d_logits = mask[:, None] * (jnp.exp(logits - log_total[:, None]) - onehot)
    head_part = jnp.dot(flat_rows.T, d_logits, precision=HIGH)
    loss_total, head_grad = lax.psum((loss_part, head_part), "ctx")
    attention_gradient = jnp.dot(d_logits, head_layer.T, precision=HIGH)
    delta_rows = jnp.sum(
        (attention_gradient * flat_rows).reshape(
            local_tokens, KEY_VALUE_HEADS, head_group, HEAD_WIDTH
        ),
        axis=-1,
    )
    attention_gradient_half = attention_gradient.astype(jnp.bfloat16).reshape(
        local_tokens, KEY_VALUE_HEADS, head_group, HEAD_WIDTH
    )

    def block_terms(key_block, value_block, k_start):
        row_count = key_block.shape[0]
        seg_k = lax.dynamic_slice_in_dim(segments, k_start, row_count)
        s = masked_scores(query_tensor_four, key_block, seg_q, seg_k, own_start, k_start)
        prob = jnp.exp(s - lse[..., None])
        prob16 = prob.astype(jnp.bfloat16)
        key_tensor_three = key_block.reshape(row_count, KEY_VALUE_HEADS, HEAD_WIDTH)
        value_tensor_three = value_block.reshape(row_count, KEY_VALUE_HEADS, HEAD_WIDTH)
        value_gradient_term = jnp.einsum(
            "tgrn,tgrd->ngd", prob16, attention_gradient_half, preferred_element_type=jnp.float32
        )
        dp = jnp.einsum(
            "tgrd,ngd->tgrn",
            attention_gradient_half,
            value_tensor_three,
            preferred_element_type=jnp.float32,
        )
        ds16 = (prob * (dp - delta_rows[..., None]) * HEAD_WIDTH ** (-0.5)).astype(jnp.bfloat16)
        query_gradient_term = jnp.einsum(
            "tgrn,ngd->tgrd", ds16, key_tensor_three, preferred_element_type=jnp.float32
        )
        key_gradient_term = jnp.einsum(
            "tgrn,tgrd->ngd", ds16, query_tensor_four, preferred_element_type=jnp.float32
        )
        return (
            key_gradient_term.reshape(row_count, KEY_VALUE_HEADS * HEAD_WIDTH),
            value_gradient_term.reshape(row_count, KEY_VALUE_HEADS * HEAD_WIDTH),
            query_gradient_term,
        )

    query_gradient_zeros = jnp.zeros(
        (local_tokens, KEY_VALUE_HEADS, head_group, HEAD_WIDTH), jnp.float32
    )
    key_all, value_all = (
        lax.all_gather(key_whole, "ctx", axis=0, tiled=True),
        lax.all_gather(value_whole, "ctx", axis=0, tiled=True),
    )
    total_rows = key_all.shape[0]

    def visit(block, carry):
        dk_buffer, dv_buffer, dq_acc = carry
        k_start = (block * local_tokens).astype(jnp.int32)

        def add(parts):
            key_block = lax.dynamic_slice_in_dim(key_all, k_start, local_tokens)
            value_block = lax.dynamic_slice_in_dim(value_all, k_start, local_tokens)
            key_gradient_term, value_gradient_term, query_gradient_term = block_terms(
                key_block, value_block, k_start
            )
            dk_old = lax.dynamic_slice_in_dim(parts[0], k_start, local_tokens)
            dv_old = lax.dynamic_slice_in_dim(parts[1], k_start, local_tokens)
            dk_new = lax.dynamic_update_slice_in_dim(
                parts[0], dk_old + key_gradient_term, k_start, 0
            )
            dv_new = lax.dynamic_update_slice_in_dim(
                parts[1], dv_old + value_gradient_term, k_start, 0
            )
            return (dk_new, dv_new, parts[2] + query_gradient_term)

        return lax.cond(
            reaches(k_start, local_tokens), add, lambda parts: parts, (dk_buffer, dv_buffer, dq_acc)
        )

    buffer_zero = jnp.zeros((total_rows, KEY_VALUE_HEADS * HEAD_WIDTH), jnp.float32)
    dk_buffer, dv_buffer, dq_acc = lax.fori_loop(
        0, n_ctx, visit, (buffer_zero, buffer_zero, query_gradient_zeros)
    )
    dk_shard, dv_shard = (
        lax.psum_scatter(
            dk_buffer.astype(jnp.bfloat16), "ctx", scatter_dimension=0, tiled=True
        ).astype(jnp.float32),
        lax.psum_scatter(
            dv_buffer.astype(jnp.bfloat16), "ctx", scatter_dimension=0, tiled=True
        ).astype(jnp.float32),
    )
    grad_keys, grad_values = (
        lax.psum_scatter(
            dk_shard.astype(jnp.bfloat16), "layer", scatter_dimension=0, tiled=True
        ).astype(jnp.float32),
        lax.psum_scatter(
            dv_shard.astype(jnp.bfloat16), "layer", scatter_dimension=0, tiled=True
        ).astype(jnp.float32),
    )
    loss = (loss_total / (local_tokens * n_ctx)).reshape(1)
    query_gradient = dq_acc.reshape(1, local_tokens, QUERY_HEADS * HEAD_WIDTH)
    return (loss, query_gradient, grad_keys, grad_values, head_grad[None])


def solution(mesh):
    return jax.shard_map(
        per_device,
        mesh=mesh,
        in_specs=(
            P("layer", "ctx", None),
            P(("ctx", "layer"), None),
            P(("ctx", "layer"), None),
            P("layer", None, None),
            P(),
            P("ctx"),
            P("ctx"),
        ),
        out_specs=(
            P("layer"),
            P("layer", "ctx", None),
            P(("ctx", "layer"), None),
            P(("ctx", "layer"), None),
            P("layer", None, None),
        ),
        check_vma=False,
    )
```

profile of v0, /device:TPU:1, one launch (start us, length us, event | category | flops | bytes accessed | tf_op | source)
XLA Modules:
  0.0 315.1 jit_solution(13078042809968540452)
XLA Ops:
  8.7 1.4 fusion.30
  11.4 25.8 %all_gather.14 = bf16[128,512]{1,0:T(8,128)(2,1)S(1)} all-gather(bf16[16,512]{1,0:T(8,128)(2,1)} %param.14), channel_id=1, replica_groups=mesh['layer'=8,'ctx'=4] {'layer'}, dimensions={0}, use_global_device_ids=true | all-gather | bytes 147456 | tf_op jit(solution)/shard_map/all_gather | solution.py:44
  37.2 24.7 %all_gather.16 = bf16[128,512]{1,0:T(8,128)(2,1)S(1)} all-gather(bf16[16,512]{1,0:T(8,128)(2,1)} %param.15), channel_id=1, replica_groups=mesh['layer'=8,'ctx'=4] {'layer'}, dimensions={0}, use_global_device_ids=true | all-gather | bytes 147456 | tf_op jit(solution)/shard_map/all_gather | solution.py:45
  61.9 19.9 %all_gather.17 = bf16[512,512]{1,0:T(8,128)(2,1)S(1)} all-gather(bf16[128,512]{1,0:T(8,128)(2,1)S(1)} %all_gather.16), channel_id=1, replica_groups=mesh['layer'=8,'ctx'=4] {'ctx'}, dimensions={0}, use_global_device_ids=true | all-gather | bytes 655360 | tf_op jit(solution)/shard_map/all_gather | solution.py:54
  81.7 7.3 %all_gather.15 = bf16[512,512]{1,0:T(8,128)(2,1)S(1)} all-gather(bf16[128,512]{1,0:T(8,128)(2,1)S(1)} %all_gather.14), channel_id=1, replica_groups=mesh['layer'=8,'ctx'=4] {'ctx'}, dimensions={0}, use_global_device_ids=true | all-gather | bytes 655360 | tf_op jit(solution)/shard_map/all_gather | solution.py:53
  89.0 1.2 copy.65
  90.2 1.0 copy.71
  91.2 1.0 copy.72
  92.3 8.3 %conditional.2 = (f32[128,4,3]{0,2,1:T(4,128)}, f32[128,4,3]{0,2,1:T(4,128)}, f32[128,4,3]{0,2,1:T(4,128)S(1)}, f32[128,4,3,128]{0,3,2,1:T(8,128)S(1)}) conditional(s32[]{:T(128)} %convert_element_type.46, () %tuple.47, (s32[]{:T(128)}, s32[512]{0:T(512)S(1)}, s32[128]{0:T(128)S(1)}, bf16[512,512]{1,0:T(8,128)(2,1)S(1)}, ...), branch_computations={%region_0.0_spmd, %region_1.4_spmd} | conditional | flops 1417345664 | bytes 15650340 | solution.py:68
  93.9 2.0 fusion.1
  95.9 3.7 %fusion.7 = f32[128,4,3,128]{3,0,2,1:T(8,128)S(1)} fusion(f32[4,512,128,3]{2,1,3,0:T(8,128)S(1)} %get-tuple-element.545, f32[128,4,3]{0,2,1:T(4,128)} %broadcast_maximum_fusion, pred[128,512]{0,1:T(8,128)(4,1)S(1)} %fusion.11, bf16[512,4,128,1]{2,1,0,3:T(4,128)(2,1)S(1)} %bitcast.109), kind=kOutput, calls=%fused_computation.9 | convolution fusion | flops 1210318848 | bytes 4528128 | tf_op jit(solution)/shard_map/cond/branch_1_fun/tgrn,ngd->tgrd/dot_general | solution.py:65
  102.8 1.6 fusion.29
  104.7 1.2 copy.68
  106.9 1.1 broadcast_in_dim.41
  108.0 18.6 %while.19 = (s32[]{:T(128)}, f32[512,512]{0,1:T(8,128)}, f32[512,512]{0,1:T(8,128)S(1)}, f32[128,4,3,128]{0,3,2,1:T(8,128)S(1)}, s32[]{:T(128)}, /*index=5*/s32[...) while((s32[]{:T(128)}, f32[512,512]{0,1:T(8,128)}, ...), condition=%wide.region_13.14_spmd, body=%wide.region_10.13_spmd.sunk | while | flops 253608208 | bytes 9748977 | solution.py:155
  109.9 5.4 %conditional.4 = ((f32[512,512]{0,1:T(8,128)}, f32[512,512]{0,1:T(8,128)S(1)}, f32[128,4,3,128]{0,3,2,1:T(8,128)S(1)})) conditional(s32[]{:T(128)} %convert_element_type.64, (f32[512,512]{0,1:T(8,128)}, f32[512,512]{0,1:T(8,128)S(1)}, f32[128,4,3,128]{0,3,2,1:T(8,128)S(1)}) %tuple.79, (s32[]{:T(128)}, f32[512,512]{0,1:T(8,128)}, s32[]{:T(128)}, ...), branch_computations={%region_11.11_spmd, %region_12.12_spmd} | conditional | flops 253608192 | bytes 9748570 | solution.py:150
  111.1 0.9 constant_dynamic-slice_fusion
  113.5 1.8 constant_dynamic-update-slice_fusion
  117.3 5.4 %conditional.4 = ((f32[512,512]{0,1:T(8,128)}, f32[512,512]{0,1:T(8,128)S(1)}, f32[128,4,3,128]{0,3,2,1:T(8,128)S(1)})) conditional(s32[]{:T(128)} %convert_element_type.64, (f32[512,512]{0,1:T(8,128)}, f32[512,512]{0,1:T(8,128)S(1)}, f32[128,4,3,128]{0,3,2,1:T(8,128)S(1)}) %tuple.79, (s32[]{:T(128)}, f32[512,512]{0,1:T(8,128)}, s32[]{:T(128)}, ...), branch_computations={%region_11.11_spmd, %region_12.12_spmd} | conditional | flops 253608192 | bytes 9748570 | solution.py:150
  117.5 0.9 constant_dynamic-slice_fusion.1
  118.4 0.9 constant_dynamic-slice_fusion
  120.9 1.8 constant_dynamic-update-slice_fusion
  126.6 2.2 copy.73
  128.9 1.0 copy.74
  130.0 25.7 %reduce-scatter.5.cloned.1.call-done = bf16[128,512]{1,0:T(8,128)(2,1)} async-done(((bf16[512,512]{1,0:T(8,128)(2,1)}), bf16[128,512]{1,0:T(8,128)(2,1)}) %reduce-scatter.5.cloned.1.call-update) | async-done | bytes 131088 | tf_op jit(solution)/shard_map/reduce_scatter | solution.py:159
  155.8 24.3 %reduce-scatter.9.cloned.1.call-done = bf16[128,512]{1,0:T(8,128)(2,1)} async-done(((bf16[512,512]{1,0:T(8,128)(2,1)}), bf16[128,512]{1,0:T(8,128)(2,1)}) %reduce-scatter.9.cloned.1.call-update) | async-done | bytes 131088 | tf_op jit(solution)/shard_map/reduce_scatter | solution.py:162
  180.9 10.3 %all-reduce = (f32[]{:T(128)}, f32[1,1536,2]{1,2,0:T(2,128)}) all-reduce(f32[]{:T(128)} %get-tuple-element.542, f32[1,1536,2]{1,2,0:T(2,128)S(1)} %convolution_bitcast_fusion.2), channel_id=1, replica_groups=mesh['layer'=8,'ctx'=4] {'ctx'}, use_global_device_ids=true, to_apply=%region_8.9 | all-reduce | flops 3073 | bytes 24584 | tf_op jit(solution)/shard_map/psum | solution.py:79
  191.2 1.1 copy.75
  193.0 49.4 %reduce-scatter.7.cloned.1.call-done = bf16[16,512]{1,0:T(8,128)(2,1)} async-done(((bf16[128,512]{1,0:T(8,128)(2,1)}), bf16[16,512]{1,0:T(8,128)(2,1)}) %reduce-scatter.7.cloned.1.call-update) | async-done | bytes 16400 | tf_op jit(solution)/shard_map/reduce_scatter | solution.py:167
  242.3 1.3 convert_element_type.50
  243.7 62.4 %reduce-scatter.11.cloned.1.call-done = bf16[16,512]{1,0:T(8,128)(2,1)} async-done(((bf16[128,512]{1,0:T(8,128)(2,1)}), bf16[16,512]{1,0:T(8,128)(2,1)}) %reduce-scatter.11.cloned.1.call-update) | async-done | bytes 16400 | tf_op jit(solution)/shard_map/reduce_scatter | solution.py:170
  306.1 1.3 convert_element_type.52
  (62 shorter events, 15.4 us)
Async XLA Ops:
  7.2 94.5 %copy-start = (f32[1,1536,2]{1,2,0:T(2,128)S(1)}, f32[1,1536,2]{1,2,0:T(2,128)}, u32[]{:S(2)}) copy-start(f32[1,1536,2]{1,2,0:T(2,128)} %param.16) | copy-start | bytes 36868
  7.2 85.1 %copy-start.1 = (s32[512]{0:T(512)S(1)}, s32[512]{0:T(512)}, u32[]{:S(2)}) copy-start(s32[512]{0:T(512)} %param.17) | copy-start | bytes 6148
  7.2 148.5 %reduce-scatter.5.cloned.1.call-start = ((), (), s32[]{:S(2)}) async-start(), calls=%async_computation.4 | async-start | bytes 655360 | tf_op jit(solution)/shard_map/reduce_scatter | solution.py:159
  100.5 1.6 copy-start.2
  100.6 1.7 copy-start.3
  128.9 51.2 %reduce-scatter.9.cloned.1.call-start = ((), (), s32[]{:S(2)}) async-start(), calls=%async_computation.6 | async-start | bytes 655360 | tf_op jit(solution)/shard_map/reduce_scatter | solution.py:162
  130.0 112.4 %reduce-scatter.7.cloned.1.call-start = ((), (), s32[]{:S(2)}) async-start(), calls=%async_computation.5 | async-start | bytes 147456 | tf_op jit(solution)/shard_map/reduce_scatter | solution.py:167
  155.8 150.3 %reduce-scatter.11.cloned.1.call-start = ((), (), s32[]{:S(2)}) async-start(), calls=%async_computation.7 | async-start | bytes 147456 | tf_op jit(solution)/shard_map/reduce_scatter | solution.py:170
Sparse Core Ops, SparseCore 0:
  129.0 26.6 reduce-scatter.4
  158.4 21.6 reduce-scatter.8
  183.4 58.9 reduce-scatter.6
  245.5 60.5 reduce-scatter.10
where the time goes:
time: 319 us; the launch traced here: 315 us
  waiting for transfers between devices  162 us (51%)
  blocking collectives  88 us (28%)
  local copies, waits for them, and re-layouts  20.5 us (6%)
  between operations  17 us (5%)
  other arithmetic  12 us (4%)
  matrix products  10.3 us (3%)
  loops' own time  5.39 us (2%)
    reduce_scatter x1, waiting for transfers between devices, per_device(): lax.psum_scatter(dv_shard.astype(jnp.bfloat16), 'layer', scatter_dimensio...  62.4 us
    reduce_scatter x1, waiting for transfers between devices, per_device(): lax.psum_scatter(dk_shard.astype(jnp.bfloat16), 'layer', scatter_dimensio...  49.4 us
    all_gather x1, blocking collectives, per_device(): lax.all_gather(keys, 'layer', axis=0, tiled=True)  25.8 us
    reduce_scatter x1, waiting for transfers between devices, per_device(): lax.psum_scatter(dk_buffer.astype(jnp.bfloat16), 'ctx', scatter_dimension...  25.7 us
    all_gather x1, blocking collectives, per_device(): lax.all_gather(values, 'layer', axis=0, tiled=True)  24.7 us
    reduce_scatter x1, waiting for transfers between devices, per_device(): lax.psum_scatter(dv_buffer.astype(jnp.bfloat16), 'ctx', scatter_dimension...  24.3 us
    all_gather x1, blocking collectives, per_device(): value_portion = lax.all_gather(value_whole, 'ctx', axis=0, tiled=True)  19.9 us
    psum x1, blocking collectives, per_device(): loss_total, head_grad = lax.psum((loss_part, head_part), 'ctx')  10.3 us
  transfers between devices with their start and end apart: 4, of which 4 were waited for; matrix products, arithmetic and copies ran while one was open for 1% of the time, Pallas kernels for 0%

commit v1 on v0

v1 whole, which is shorter than its diff:
```python
import functools

import jax
import jax.numpy as jnp
from jax import lax
from jax.experimental import pallas as pl
from jax.experimental.pallas import tpu as pltpu
from jax.sharding import PartitionSpec as P

QUERY_HEADS = 12
KEY_VALUE_HEADS = 4
HEAD_WIDTH = 128

GROUP = QUERY_HEADS // KEY_VALUE_HEADS
LOG2_E = 1.4426950408889634
NEGATIVE_FILL = -1e30
HIGH = lax.Precision.HIGHEST
MESH = pl.DeviceIdType.MESH
STAT_ROWS = 8


def dot(a, b, a_dim, b_dim, precision=None):
    return lax.dot_general(
        a, b, (((a_dim,), (b_dim,)), ((), ())), precision=precision,
        preferred_element_type=jnp.float32,
    )


def kernel(
    n_layer, n_ctx, q_ref, k_ref, v_ref, head_ref, seg_ref, mask_ref, label_ref,
    loss_ref, dq_ref, gk_ref, gv_ref, hg_ref,
    kv, score, hb, peak, total, att, datt, delta, dqt, grad, stats,
    send_ctx, recv_ctx, send_x, recv_x, send_z, recv_z,
    gz_s, gz_r, gx_s, gx_r, gc_s, gc_r, st_s, st_r, rc_s, rc_r, rx_s, rx_r, rz_s, rz_r,
):
    W = HEAD_WIDTH
    local = q_ref.shape[0]
    rows = k_ref.shape[0]
    classes = head_ref.shape[0]
    n_high = n_layer // 2
    layer, ctx = lax.axis_index("layer"), lax.axis_index("ctx")
    high, low = layer // 2, layer % 2
    twin = high * 2 + (1 - low)
    tail = (3 * n_ctx) // 4
    in_tail = (ctx >= tail).astype(jnp.int32)
    first = in_tail * tail
    end = tail + in_tail * (n_ctx - tail)
    count = ctx - first + 1

    def remote(src, dst, s, r, to_layer, to_ctx):
        return pltpu.make_async_remote_copy(
            src_ref=src, dst_ref=dst, send_sem=s, recv_sem=r,
            device_id=(to_layer, to_ctx), device_id_type=MESH,
        )

    kv[ctx, layer, 0] = k_ref[...]
    kv[ctx, layer, 1] = v_ref[...]

    barrier = pltpu.get_barrier_semaphore()
    for d in range(1, n_high):
        pl.semaphore_signal(
            barrier, inc=1, device_id=(lax.rem(high + d, n_high) * 2 + low, ctx),
            device_id_type=MESH)
    pl.semaphore_signal(barrier, inc=1, device_id=(twin, ctx), device_id_type=MESH)
    for d in range(1, n_ctx):
        pl.semaphore_signal(
            barrier, inc=1, device_id=(layer, lax.rem(ctx + d, n_ctx)), device_id_type=MESH)
    pl.semaphore_wait(barrier, n_high + n_ctx - 1)

    def to_later(piece):
        def one(to, carry):
            remote(kv.at[ctx, piece], kv.at[ctx, piece], gc_s.at[to], gc_r.at[ctx],
                   layer, to).start()
            return carry
        lax.fori_loop(ctx + 1, end, one, 0)

    def line_copy(d):
        return remote(kv.at[ctx, layer], kv.at[ctx, layer], gz_s.at[d], gz_r.at[d],
                      lax.rem(high + d, n_high) * 2 + low, ctx)

    def twin_copy(d, side):
        piece = lax.rem(high + n_high - d, n_high) * 2 + side
        return remote(kv.at[ctx, piece], kv.at[ctx, piece], gx_s.at[d], gx_r.at[d], twin, ctx)

    for d in range(1, n_high):
        line_copy(d).start()
    twin_copy(0, low).start()
    to_later(layer)

    for k in range(classes):
        for h in range(QUERY_HEADS):
            row = head_ref[k : k + 1, h * W : (h + 1) * W]
            hb[k, h] = jnp.transpose(jnp.broadcast_to(row, (local, W)))

    for d in range(1, n_high):
        piece = lax.rem(high + n_high - d, n_high) * 2 + low
        remote(kv.at[ctx, piece], kv.at[ctx, piece], gz_s.at[d], gz_r.at[d],
               layer, ctx).wait_recv()
        twin_copy(d, low).start()
        to_later(piece)
    for d in range(n_high):
        twin_copy(d, 1 - low).wait_recv()
        to_later(lax.rem(high + n_high - d, n_high) * 2 + (1 - low))

    def block_of(j, which, g):
        part = kv[j, :, which, :, g * W : (g + 1) * W]
        if rows % 16:
            return part.astype(jnp.float32).reshape(n_layer * rows, W).astype(jnp.bfloat16)
        return part.reshape(n_layer * rows, W)

    def query_of(g):
        return jnp.concatenate(
            [q_ref[:, (g * GROUP + r) * W : (g * GROUP + r + 1) * W] for r in range(GROUP)], axis=0)

    peak[...] = jnp.full_like(peak, NEGATIVE_FILL)
    total[...] = jnp.zeros_like(total)
    att[...] = jnp.zeros_like(att)
    dqt[...] = jnp.zeros_like(dqt)

    seg_q = seg_ref[pl.ds(ctx, 1), :]

    def score_block(i, carry):
        j = ctx - i

        @pl.when(i > 0)
        def _():
            remote(kv.at[j], kv.at[j], gc_s.at[j], gc_r.at[j], layer, ctx).wait_recv()

        seg_k = jnp.transpose(
            jnp.broadcast_to(seg_ref[pl.ds(j, 1), :], (local, local)).astype(jnp.float32))
        same = seg_k == jnp.broadcast_to(seg_q, (local, local)).astype(jnp.float32)
        k_pos = j * local + lax.broadcasted_iota(jnp.int32, (local, local), 0)
        q_pos = ctx * local + lax.broadcasted_iota(jnp.int32, (local, local), 1)
        fill = jnp.where(same & (k_pos <= q_pos), 0.0, NEGATIVE_FILL)
        fill = jnp.concatenate([fill] * GROUP, axis=1)
        for g in range(KEY_VALUE_HEADS):
            s = dot(block_of(j, 0, g), query_of(g), 1, 1) * (LOG2_E * W ** -0.5)
            s = jnp.where(fill < 0.0, NEGATIVE_FILL, s)
            score[j, g] = s
            peak[g] = jnp.maximum(peak[g], jnp.max(s, axis=0, keepdims=True))
        return carry

    lax.fori_loop(0, count, score_block, 0)

    def weigh_block(i, carry):
        j = ctx - i
        for g in range(KEY_VALUE_HEADS):
            p = jnp.exp2(score[j, g] - peak[g])
            score[j, g] = p
            total[g] += jnp.sum(p, axis=0, keepdims=True)
            att[g] += dot(block_of(j, 1, g), p.astype(jnp.bfloat16), 0, 0)
        return carry

    lax.fori_loop(0, count, weigh_block, 0)

    logits = [jnp.zeros((1, local), jnp.float32) for _ in range(classes)]
    parts = []
    for g in range(KEY_VALUE_HEADS):
        inverse = 1.0 / total[g]
        total[g] = inverse
        att[g] = att[g] * inverse
        for r in range(GROUP):
            a = att[g, :, r * W : (r + 1) * W]
            part = [jnp.sum(hb[k, g * GROUP + r] * a, axis=0, keepdims=True)
                    for k in range(classes)]
            parts.append(part)
            logits = [x + y for x, y in zip(logits, part)]
    biggest = functools.reduce(jnp.maximum, logits)
    log_total = biggest + jnp.log(sum(jnp.exp(x - biggest) for x in logits))
    mask = mask_ref[...].astype(jnp.float32)
    hot = [(label_ref[...] == k).astype(jnp.float32) for k in range(classes)]
    loss_rows = mask * (log_total - sum(o * x for o, x in zip(hot, logits)))
    d_logits = [mask * (jnp.exp(x - log_total) - o) for o, x in zip(hot, logits)]

    stacked = jnp.concatenate(
        d_logits + [jnp.zeros((STAT_ROWS - classes, local), jnp.float32)], axis=0)
    for h in range(QUERY_HEADS):
        g, r = h // GROUP, h % GROUP
        cols = slice(r * W, (r + 1) * W)
        stats[ctx, :, h * W : (h + 1) * W] = dot(stacked, att[g, :, cols], 1, 1, HIGH)
        da = sum(hb[k, h] * d_logits[k] for k in range(classes))
        datt[g, :, cols] = da.astype(jnp.bfloat16)
        delta[g, :, cols] = sum(parts[h][k] * d_logits[k] for k in range(classes))
    stats[ctx, classes : classes + 1, 0:local] = loss_rows

    for d in range(1, n_ctx):
        remote(stats.at[ctx], stats.at[ctx], st_s.at[d], st_r.at[d],
               layer, lax.rem(ctx + d, n_ctx)).start()

    def back_block(i, carry):
        j = first + i
        for g in range(KEY_VALUE_HEADS):
            k_block, v_block = block_of(j, 0, g), block_of(j, 1, g)
            da = datt[g]
            dp = dot(v_block, da, 1, 0)
            prob = score[j, g] * total[g]
            ds = (prob * ((dp - delta[g]) * W ** -0.5)).astype(jnp.bfloat16)
            dqt[g] += dot(k_block, ds, 0, 0)
            cols = slice(g * W, (g + 1) * W)
            grad[:, 0, :, cols] = dot(ds, query_of(g), 1, 0).reshape(n_layer, rows, W)
            grad[:, 1, :, cols] = dot(prob.astype(jnp.bfloat16), da, 1, 1).reshape(
                n_layer, rows, W)

        @pl.when(j < ctx)
        def _():
            send_ctx[j] = grad[...].astype(jnp.bfloat16)
            remote(send_ctx.at[j], recv_ctx.at[ctx], rc_s.at[j], rc_r.at[ctx], layer, j).start()

        return carry

    lax.fori_loop(0, count, back_block, 0)

    def gather_later(i, carry):
        remote(send_ctx.at[i], recv_ctx.at[i], rc_s.at[i], rc_r.at[i], layer, ctx).wait_recv()
        grad[...] = grad[...] + recv_ctx[i].astype(jnp.float32)
        return carry

    lax.fori_loop(ctx + 1, end, gather_later, 0)

    for z in range(n_high):
        send_x[z] = grad[z * 2 + (1 - low)].astype(jnp.bfloat16)
    x_copy = remote(send_x, recv_x, rx_s, rx_r, twin, ctx)
    x_copy.start()

    for h in range(QUERY_HEADS):
        g, r = h // GROUP, h % GROUP
        dq_ref[:, h * W : (h + 1) * W] = jnp.transpose(dqt[g, :, r * W : (r + 1) * W])

    x_copy.wait_recv()
    z_copies = []
    for d in range(1, n_high):
        to = lax.rem(high + d, n_high)
        send_z[d] = (grad[to * 2 + low] + recv_x[to].astype(jnp.float32)).astype(jnp.bfloat16)
        copy = remote(send_z.at[d], recv_z.at[d], rz_s.at[d], rz_r.at[d], to * 2 + low, ctx)
        copy.start()
        z_copies.append(copy)
    mine = grad[high * 2 + low] + recv_x[high].astype(jnp.float32)

    for d in range(1, n_ctx):
        origin = lax.rem(ctx + n_ctx - d, n_ctx)
        remote(stats.at[origin], stats.at[origin], st_s.at[d], st_r.at[d],
               layer, ctx).wait_recv()
    whole = stats[0]
    for j in range(1, n_ctx):
        whole = whole + stats[j]
    hg_ref[...] = whole[0:classes]
    loss_ref[0] = jnp.sum(whole[classes : classes + 1, 0:local]) * (1.0 / (local * n_ctx))

    for d in range(1, n_high):
        z_copies[d - 1].wait_recv()
        mine = mine + recv_z[d].astype(jnp.float32)
    gk_ref[...] = mine[0]
    gv_ref[...] = mine[1]

    for d in range(1, n_high):
        line_copy(d).wait_send()
        z_copies[d - 1].wait_send()
    for d in range(n_high):
        twin_copy(d, low).wait_send()
    for d in range(1, n_ctx):
        remote(stats.at[ctx], stats.at[ctx], st_s.at[d], st_r.at[d],
               layer, lax.rem(ctx + d, n_ctx)).wait_send()
    x_copy.wait_send()

    def sent_later(to, carry):
        remote(kv.at[ctx], kv.at[ctx], gc_s.at[to], gc_r.at[ctx], layer, to).wait_send()
        return carry

    lax.fori_loop(ctx + 1, end, sent_later, 0)

    def sent_back(j, carry):
        remote(send_ctx.at[j], recv_ctx.at[ctx], rc_s.at[j], rc_r.at[ctx], layer, j).wait_send()
        return carry

    lax.fori_loop(first, ctx, sent_back, 0)


def per_device(queries, keys, values, head, segments, label_mask, labels):
    n_layer, n_ctx = lax.axis_size("layer"), lax.axis_size("ctx")
    local, width = queries.shape[1:]
    rows, kv_width = keys.shape
    classes = head.shape[2]
    n_high = n_layer // 2
    G, W, T = KEY_VALUE_HEADS, HEAD_WIDTH, GROUP * local
    vmem = pl.BlockSpec(memory_space=pltpu.VMEM)
    bf, f32 = jnp.bfloat16, jnp.float32
    dma = pltpu.SemaphoreType.DMA
    loss, dq, gk, gv, hg = pl.pallas_call(
        functools.partial(kernel, n_layer, n_ctx),
        out_shape=(
            jax.ShapeDtypeStruct((1,), f32),
            jax.ShapeDtypeStruct((local, width), f32),
            jax.ShapeDtypeStruct((rows, kv_width), f32),
            jax.ShapeDtypeStruct((rows, kv_width), f32),
            jax.ShapeDtypeStruct((classes, width), f32),
        ),
        in_specs=[vmem] * 7,
        out_specs=(pl.BlockSpec(memory_space=pltpu.SMEM), vmem, vmem, vmem, vmem),
        scratch_shapes=[
            pltpu.VMEM((n_ctx, n_layer, 2, rows, kv_width), bf),
            pltpu.VMEM((n_ctx, G, local, T), f32),
            pltpu.VMEM((classes, QUERY_HEADS, W, local), f32),
            pltpu.VMEM((G, 1, T), f32),
            pltpu.VMEM((G, 1, T), f32),
            pltpu.VMEM((G, W, T), f32),
            pltpu.VMEM((G, W, T), bf),
            pltpu.VMEM((G, 1, T), f32),
            pltpu.VMEM((G, W, T), f32),
            pltpu.VMEM((n_layer, 2, rows, kv_width), f32),
            pltpu.VMEM((n_ctx, STAT_ROWS, width), f32),
            pltpu.VMEM((n_ctx, n_layer, 2, rows, kv_width), bf),
            pltpu.VMEM((n_ctx, n_layer, 2, rows, kv_width), bf),
            pltpu.VMEM((n_high, 2, rows, kv_width), bf),
            pltpu.VMEM((n_high, 2, rows, kv_width), bf),
            pltpu.VMEM((n_high, 2, rows, kv_width), bf),
            pltpu.VMEM((n_high, 2, rows, kv_width), bf),
            dma((n_high,)), dma((n_high,)), dma((n_high,)), dma((n_high,)),
            dma((n_ctx,)), dma((n_ctx,)), dma((n_ctx,)), dma((n_ctx,)),
            dma((n_ctx,)), dma((n_ctx,)), dma, dma,
            dma((n_high,)), dma((n_high,)),
        ],
        compiler_params=pltpu.CompilerParams(
            collective_id=0, has_side_effects=True, vmem_limit_bytes=48 * 1024 * 1024),
    )(
        queries[0], keys, values, jnp.swapaxes(head[0], 0, 1),
        segments.reshape(n_ctx, local), label_mask[None], labels[None],
    )
    return loss, dq[None], gk, gv, jnp.swapaxes(hg, 0, 1)[None]


def solution(mesh):
    return jax.shard_map(
        per_device,
        mesh=mesh,
        in_specs=(
            P("layer", "ctx", None),
            P(("ctx", "layer"), None),
            P(("ctx", "layer"), None),
            P("layer", None, None),
            P(),
            P("ctx"),
            P("ctx"),
        ),
        out_specs=(
            P("layer"),
            P("layer", "ctx", None),
            P(("ctx", "layer"), None),
            P(("ctx", "layer"), None),
            P("layer", None, None),
        ),
        check_vma=False,
    )
```

time: 319 us -> 44.1 us (0.14); the launches traced: 315 us -> 43.6 us
  waiting for transfers between devices: 162 us -> 0 us
  blocking collectives: 88 us -> 0 us
  Pallas kernels: 0 us -> 34.7 us
  between operations: 17 us -> 2.36 us
  local copies, waits for them, and re-layouts: 20.5 us -> 6.51 us
  other arithmetic: 12 us -> 0 us
  matrix products: 10.3 us -> 0 us
  loops' own time: 5.39 us -> 0 us
    reduce_scatter x4 -> x0, waiting for transfers between devices: 162 us -> none  [the longest x1 62.4 us: per_device(): lax.psum_scatter(dv_shard.astype(jnp.bfloat16), 'layer', scatter_dimensio...]
    all_gather x4 -> x0, blocking collectives: 77.7 us -> none  [the longest x1 25.8 us: per_device(): lax.all_gather(keys, 'layer', axis=0, tiled=True)]
    pallas_call x0 -> x1, Pallas kernels: none -> 34.7 us  [per_device(): pl.pallas_call(functools.partial(kernel, n_layer, n_ctx), out_shape=(jax....]
    psum x1 -> x0, blocking collectives: 10.3 us -> none  [per_device(): loss_total, head_grad = lax.psum((loss_part, head_part), 'ctx')]
    dot_general x15 -> x0, matrix products: 10.3 us -> none  [the longest x1 3.67 us: update(): jnp.einsum('tgrn,ngd->tgrd', weights, value_tensor_three, precision=HIGH)]
    dynamic_slice x12 -> x0, local copies, waits for them, and re-layouts: 8.59 us -> none  [the longest x4 2.59 us: reaches(): segments[jnp.maximum(last, 0)] >= segments[own_start]]
    another operation x6 -> x0, loops' own time: 5.39 us -> none  [the longest x1 5.18 us: per_device(): lax.fori_loop(0, n_ctx, visit, (buffer_zero, buffer_zero, query_gradient_...]
    while x4 -> x0, local copies, waits for them, and re-layouts: 5.26 us -> none  [per_device(): lax.fori_loop(0, n_ctx, visit, (buffer_zero, buffer_zero, query_gradient_...]
  transfers between devices with their start and end apart: 4 -> 0, of which waited for: 4 -> 0; matrix products, arithmetic and copies ran while one was open for 1% -> 0% of each run, Pallas kernels for 0% -> 0%
where the time goes in v1:
time: 44.1 us; the launch traced here: 43.6 us
  Pallas kernels  34.7 us (79%)
  local copies, waits for them, and re-layouts  6.51 us (15%)
  between operations  2.36 us (5%)
    pallas_call x1, Pallas kernels, per_device(): pl.pallas_call(functools.partial(kernel, n_layer, n_ctx), out_shape=(jax....  34.7 us
    unnamed x18, local copies, waits for them, and re-layouts  6.51 us

profile of v1, /device:TPU:1, one launch (start us, length us, event | category | flops | bytes accessed | tf_op | source)
XLA Modules:
  0.0 43.6 jit_solution(6286307460202319088)
XLA Ops:
  0.6 0.0 copy-start.4
  0.6 0.0 copy-start.5
  0.7 0.0 copy-start.6
  0.7 0.7 %copy-done.4 = s32[512]{0:T(512)S(1)} copy-done((s32[512]{0:T(512)S(1)}, s32[512]{0:T(512)}, u32[]{:S(2)}) %copy-start.4) | copy-done | bytes 2072
  1.3 0.0 copy-done.5
  1.3 0.0 copy-done.6
  1.3 0.0 copy-start
  1.3 1.0 %copy-done = bf16[1,128,1536]{2,1,0:T(8,128)(2,1)S(1)} copy-done((bf16[1,128,1536]{2,1,0:T(8,128)(2,1)S(1)}, bf16[1,128,1536]{2,1,0:T(8,128)(2,1)}, u32[]{:S(2)}) %copy-start) | copy-done | bytes 393240
  2.3 0.0 copy-start.1
  2.3 0.7 %copy-done.1 = bf16[16,512]{1,0:T(8,128)(2,1)S(1)} copy-done((bf16[16,512]{1,0:T(8,128)(2,1)S(1)}, bf16[16,512]{1,0:T(8,128)(2,1)}, u32[]{:S(2)}) %copy-start.1) | copy-done | bytes 16408
  3.0 0.0 copy-start.2
  3.0 0.7 %copy-done.2 = bf16[16,512]{1,0:T(8,128)(2,1)S(1)} copy-done((bf16[16,512]{1,0:T(8,128)(2,1)S(1)}, bf16[16,512]{1,0:T(8,128)(2,1)}, u32[]{:S(2)}) %copy-start.2) | copy-done | bytes 16408
  3.8 0.0 copy-start.3
  3.8 0.7 %copy-done.3 = f32[1,1536,2]{1,2,0:T(2,128)S(1)} copy-done((f32[1,1536,2]{1,2,0:T(2,128)S(1)}, f32[1,1536,2]{1,2,0:T(2,128)}, u32[]{:S(2)}) %copy-start.3) | copy-done | bytes 12312
  4.5 34.7 %shard_map.110 = (f32[1]{0:T(128)}, f32[128,1536]{1,0:T(8,128)S(1)}, f32[16,512]{1,0:T(8,128)S(1)}, f32[16,512]{1,0:T(8,128)S(1)}, f32[2,1536]{1,0:T(2,128)S(1)}) custom-call(bf16[128,1536]{1,0:T(8,128)(2,1)S(1)} %bitcast.12, bf16[16,512]{1,0:T(8,128)(2,1)S(1)} %copy-done.1, bf16[16,512]{1,0:T(8,128)(2,1)S(1)} %copy-done.2, f32[2,1536]{1,0:T(2,128)S(1)} %bitcast.13, ...), custom_call_target="tpu_custom_call" | custom-call | tf_op jit(solution)/shard_map/pallas_call | solution.py:288
  39.8 0.9 %copy.18 = f32[1,128,1536]{2,1,0:T(8,128)} copy(f32[1,128,1536]{2,1,0:T(8,128)S(1)} %bitcast.11) | data formatting | bytes 1572864
  40.6 0.6 %copy.19 = f32[16,512]{1,0:T(8,128)} copy(f32[16,512]{1,0:T(8,128)S(1)} %get-tuple-element.22) | data formatting | bytes 65536
  41.3 0.6 %copy.20 = f32[16,512]{1,0:T(8,128)} copy(f32[16,512]{1,0:T(8,128)S(1)} %get-tuple-element.23) | data formatting | bytes 65536
  41.9 0.6 %copy.21 = f32[1,1536,2]{1,2,0:T(2,128)} copy(f32[1,1536,2]{1,2,0:T(2,128)S(1)} %bitcast.14) | data formatting | bytes 24576
Async XLA Ops:
  0.6 0.7 %copy-start.4 = (s32[512]{0:T(512)S(1)}, s32[512]{0:T(512)}, u32[]{:S(2)}) copy-start(s32[512]{0:T(512)} %param.11) | copy-start | bytes 6148
  0.6 0.7 %copy-start.5 = (s32[128]{0:T(128)S(1)}, s32[128]{0:T(128)}, u32[]{:S(2)}) copy-start(s32[128]{0:T(128)} %param.12) | copy-start | bytes 1540
  0.7 0.7 %copy-start.6 = (s32[128]{0:T(128)S(1)}, s32[128]{0:T(128)}, u32[]{:S(2)}) copy-start(s32[128]{0:T(128)} %param.13) | copy-start | bytes 1540
  1.3 1.0 %copy-start = (bf16[1,128,1536]{2,1,0:T(8,128)(2,1)S(1)}, bf16[1,128,1536]{2,1,0:T(8,128)(2,1)}, u32[]{:S(2)}) copy-start(bf16[1,128,1536]{2,1,0:T(8,128)(2,1)} %param.7) | copy-start | bytes 1179652
  2.3 0.7 %copy-start.1 = (bf16[16,512]{1,0:T(8,128)(2,1)S(1)}, bf16[16,512]{1,0:T(8,128)(2,1)}, u32[]{:S(2)}) copy-start(bf16[16,512]{1,0:T(8,128)(2,1)} %k_ref.1) | copy-start | bytes 49156
  3.0 0.7 %copy-start.2 = (bf16[16,512]{1,0:T(8,128)(2,1)S(1)}, bf16[16,512]{1,0:T(8,128)(2,1)}, u32[]{:S(2)}) copy-start(bf16[16,512]{1,0:T(8,128)(2,1)} %v_ref.1) | copy-start | bytes 49156
  3.8 0.7 %copy-start.3 = (f32[1,1536,2]{1,2,0:T(2,128)S(1)}, f32[1,1536,2]{1,2,0:T(2,128)}, u32[]{:S(2)}) copy-start(f32[1,1536,2]{1,2,0:T(2,128)} %param.10) | copy-start | bytes 36868

commit v2 on v1

--- a/solution.py
+++ b/solution.py
@@ -27,15 +27,16 @@
 
 
 def kernel(
-    n_layer, n_ctx, q_ref, k_ref, v_ref, head_ref, seg_ref, mask_ref, label_ref,
+    n_layer, n_ctx, q_in, k_in, v_in, head_in, seg_in, mask_in, label_in,
     loss_ref, dq_ref, gk_ref, gv_ref, hg_ref,
-    kv, score, hb, peak, total, att, datt, delta, dqt, grad, stats,
+    q_ref, head_ref, seg_ref, mask_ref, label_ref, in_sem,
+    kv, score, hb, peak, tops, total, att, datt, delta, dqt, grad, mine, rows_d, stats,
     send_ctx, recv_ctx, send_x, recv_x, send_z, recv_z,
     gz_s, gz_r, gx_s, gx_r, gc_s, gc_r, st_s, st_r, rc_s, rc_r, rx_s, rx_r, rz_s, rz_r,
 ):
     W = HEAD_WIDTH
     local = q_ref.shape[0]
-    rows = k_ref.shape[0]
+    rows = k_in.shape[0]
     classes = head_ref.shape[0]
     n_high = n_layer // 2
     layer, ctx = lax.axis_index("layer"), lax.axis_index("ctx")
@@ -53,8 +54,14 @@
             device_id=(to_layer, to_ctx), device_id_type=MESH,
         )
 
-    kv[ctx, layer, 0] = k_ref[...]
-    kv[ctx, layer, 1] = v_ref[...]
+    k_load, v_load, head_load, q_load, *small_loads = [
+        pltpu.make_async_copy(src, dst, in_sem.at[i])
+        for i, (src, dst) in enumerate([
+            (k_in, kv.at[ctx, layer, 0]), (v_in, kv.at[ctx, layer, 1]), (head_in, head_ref),
+            (q_in, q_ref), (seg_in, seg_ref), (mask_in, mask_ref), (label_in, label_ref)])
+    ]
+    for load in (k_load, v_load, head_load, q_load, *small_loads):
+        load.start()
 
     barrier = pltpu.get_barrier_semaphore()
     for d in range(1, n_high):
@@ -65,6 +72,14 @@
     for d in range(1, n_ctx):
         pl.semaphore_signal(
             barrier, inc=1, device_id=(layer, lax.rem(ctx + d, n_ctx)), device_id_type=MESH)
+    head_load.wait()
+    for k in range(classes):
+        for h in range(QUERY_HEADS):
+            row = head_ref[k : k + 1, h * W : (h + 1) * W]
+            hb[k, h] = jnp.transpose(jnp.broadcast_to(row, (local, W)))
+
+    k_load.wait()
+    v_load.wait()
     pl.semaphore_wait(barrier, n_high + n_ctx - 1)
 
     def to_later(piece):
@@ -86,11 +101,6 @@
         line_copy(d).start()
     twin_copy(0, low).start()
     to_later(layer)
-
-    for k in range(classes):
-        for h in range(QUERY_HEADS):
-            row = head_ref[k : k + 1, h * W : (h + 1) * W]
-            hb[k, h] = jnp.transpose(jnp.broadcast_to(row, (local, W)))
 
     for d in range(1, n_high):
         piece = lax.rem(high + n_high - d, n_high) * 2 + low
@@ -117,6 +127,8 @@
     att[...] = jnp.zeros_like(att)
     dqt[...] = jnp.zeros_like(dqt)
 
+    for load in (q_load, *small_loads):
+        load.wait()
     seg_q = seg_ref[pl.ds(ctx, 1), :]
 
     def score_block(i, carry):
@@ -136,22 +148,17 @@
         for g in range(KEY_VALUE_HEADS):
             s = dot(block_of(j, 0, g), query_of(g), 1, 1) * (LOG2_E * W ** -0.5)
             s = jnp.where(fill < 0.0, NEGATIVE_FILL, s)
-            score[j, g] = s
-            peak[g] = jnp.maximum(peak[g], jnp.max(s, axis=0, keepdims=True))
+            top = jnp.maximum(peak[g], jnp.max(s, axis=0, keepdims=True))
+            fade = jnp.exp2(peak[g] - top)
+            p = jnp.exp2(s - top)
+            score[j, g] = p
+            tops[j, g] = top
+            peak[g] = top
+            total[g] = total[g] * fade + jnp.sum(p, axis=0, keepdims=True)
+            att[g] = att[g] * fade + dot(block_of(j, 1, g), p.astype(jnp.bfloat16), 0, 0)
         return carry
 
     lax.fori_loop(0, count, score_block, 0)
-
-    def weigh_block(i, carry):
-        j = ctx - i
-        for g in range(KEY_VALUE_HEADS):
-            p = jnp.exp2(score[j, g] - peak[g])
-            score[j, g] = p
-            total[g] += jnp.sum(p, axis=0, keepdims=True)
-            att[g] += dot(block_of(j, 1, g), p.astype(jnp.bfloat16), 0, 0)
-        return carry
-
-    lax.fori_loop(0, count, weigh_block, 0)
 
     logits = [jnp.zeros((1, local), jnp.float32) for _ in range(classes)]
     parts = []
@@ -172,20 +179,15 @@
     loss_rows = mask * (log_total - sum(o * x for o, x in zip(hot, logits)))
     d_logits = [mask * (jnp.exp(x - log_total) - o) for o, x in zip(hot, logits)]
 
-    stacked = jnp.concatenate(
-        d_logits + [jnp.zeros((STAT_ROWS - classes, local), jnp.float32)], axis=0)
     for h in range(QUERY_HEADS):
         g, r = h // GROUP, h % GROUP
         cols = slice(r * W, (r + 1) * W)
-        stats[ctx, :, h * W : (h + 1) * W] = dot(stacked, att[g, :, cols], 1, 1, HIGH)
         da = sum(hb[k, h] * d_logits[k] for k in range(classes))
         datt[g, :, cols] = da.astype(jnp.bfloat16)
         delta[g, :, cols] = sum(parts[h][k] * d_logits[k] for k in range(classes))
-    stats[ctx, classes : classes + 1, 0:local] = loss_rows
-
-    for d in range(1, n_ctx):
-        remote(stats.at[ctx], stats.at[ctx], st_s.at[d], st_r.at[d],
-               layer, lax.rem(ctx + d, n_ctx)).start()
+    for k in range(classes):
+        rows_d[k : k + 1, :] = d_logits[k]
+    rows_d[classes : classes + 1, :] = loss_rows
 
     def back_block(i, carry):
         j = first + i
@@ -193,7 +195,7 @@
             k_block, v_block = block_of(j, 0, g), block_of(j, 1, g)
             da = datt[g]
             dp = dot(v_block, da, 1, 0)
-            prob = score[j, g] * total[g]
+            prob = score[j, g] * (total[g] * jnp.exp2(tops[j, g] - peak[g]))
             ds = (prob * ((dp - delta[g]) * W ** -0.5)).astype(jnp.bfloat16)
             dqt[g] += dot(k_block, ds, 0, 0)
             cols = slice(g * W, (g + 1) * W)
@@ -204,37 +206,78 @@
         @pl.when(j < ctx)
         def _():
             send_ctx[j] = grad[...].astype(jnp.bfloat16)
-            remote(send_ctx.at[j], recv_ctx.at[ctx], rc_s.at[j], rc_r.at[ctx], layer, j).start()
+            for d in range(n_high):
+                part = pl.ds(lax.rem(high + 1 + d, n_high) * 2, 2)
+                remote(send_ctx.at[j, part], recv_ctx.at[ctx, part], rc_s.at[j],
+                       rc_r.at[ctx, d], layer, j).start()
 
         return carry
 
     lax.fori_loop(0, count, back_block, 0)
 
-    def gather_later(i, carry):
-        remote(send_ctx.at[i], recv_ctx.at[i], rc_s.at[i], rc_r.at[i], layer, ctx).wait_recv()
-        grad[...] = grad[...] + recv_ctx[i].astype(jnp.float32)
-        return carry
-
-    lax.fori_loop(ctx + 1, end, gather_later, 0)
-
-    for z in range(n_high):
-        send_x[z] = grad[z * 2 + (1 - low)].astype(jnp.bfloat16)
-    x_copy = remote(send_x, recv_x, rx_s, rx_r, twin, ctx)
-    x_copy.start()
-
-    for h in range(QUERY_HEADS):
-        g, r = h // GROUP, h % GROUP
-        dq_ref[:, h * W : (h + 1) * W] = jnp.transpose(dqt[g, :, r * W : (r + 1) * W])
-
-    x_copy.wait_recv()
-    z_copies = []
-    for d in range(1, n_high):
-        to = lax.rem(high + d, n_high)
-        send_z[d] = (grad[to * 2 + low] + recv_x[to].astype(jnp.float32)).astype(jnp.bfloat16)
-        copy = remote(send_z.at[d], recv_z.at[d], rz_s.at[d], rz_r.at[d], to * 2 + low, ctx)
-        copy.start()
-        z_copies.append(copy)
-    mine = grad[high * 2 + low] + recv_x[high].astype(jnp.float32)
+    def side_work():
+        stacked = jnp.concatenate(
+            [rows_d[0:classes, :], jnp.zeros((STAT_ROWS - classes, local), jnp.float32)], axis=0)
+        for h in range(QUERY_HEADS):
+            g, r = h // GROUP, h % GROUP
+            stats[ctx, :, h * W : (h + 1) * W] = dot(
+                stacked, att[g, :, r * W : (r + 1) * W], 1, 1, HIGH)
+        stats[ctx, classes : classes + 1, 0:local] = rows_d[classes : classes + 1, :]
+        for d in range(1, n_ctx):
+            remote(stats.at[ctx], stats.at[ctx], st_s.at[d], st_r.at[d],
+                   layer, lax.rem(ctx + d, n_ctx)).start()
+        for h in range(QUERY_HEADS):
+            g, r = h // GROUP, h % GROUP
+            dq_ref[:, h * W : (h + 1) * W] = jnp.transpose(dqt[g, :, r * W : (r + 1) * W])
+
+    def place(d):
+        return lax.rem(high + 1 + d, n_high)
+
+    def x_copy(d):
+        return remote(send_x.at[d], recv_x.at[d], rx_s.at[d], rx_r.at[d], twin, ctx)
+
+    def z_copy(d):
+        return remote(send_z.at[d], recv_z.at[d], rz_s.at[d], rz_r.at[d],
+                      place(d) * 2 + low, ctx)
+
+    def x_stage(d):
+        part = pl.ds(place(d) * 2, 2)
+
+        def one(i, carry):
+            remote(send_ctx.at[i, part], recv_ctx.at[i, part], rc_s.at[i], rc_r.at[i, d],
+                   layer, ctx).wait_recv()
+            grad[part] = grad[part] + recv_ctx[i, part].astype(jnp.float32)
+            return carry
+
+        lax.fori_loop(ctx + 1, end, one, 0)
+        send_x[d] = grad[place(d) * 2 + (1 - low)].astype(jnp.bfloat16)
+        x_copy(d).start()
+
+    def z_stage(d):
+        x_copy(d).wait_recv()
+        value = grad[place(d) * 2 + low] + recv_x[d].astype(jnp.float32)
+        if d < n_high - 1:
+            send_z[d] = value.astype(jnp.bfloat16)
+            z_copy(d).start()
+        else:
+            mine[...] = value
+
+    @pl.when(ctx < end - 1)
+    def _():
+        side_work()
+        for d in range(n_high):
+            x_stage(d)
+            if d:
+                z_stage(d - 1)
+        z_stage(n_high - 1)
+
+    @pl.when(ctx == end - 1)
+    def _():
+        for d in range(n_high):
+            x_stage(d)
+        side_work()
+        for d in range(n_high):
+            z_stage(d)
 
     for d in range(1, n_ctx):
         origin = lax.rem(ctx + n_ctx - d, n_ctx)
@@ -246,21 +289,23 @@
     hg_ref[...] = whole[0:classes]
     loss_ref[0] = jnp.sum(whole[classes : classes + 1, 0:local]) * (1.0 / (local * n_ctx))
 
-    for d in range(1, n_high):
-        z_copies[d - 1].wait_recv()
-        mine = mine + recv_z[d].astype(jnp.float32)
-    gk_ref[...] = mine[0]
-    gv_ref[...] = mine[1]
+    result = mine[...]
+    for d in range(n_high - 1):
+        z_copy(d).wait_recv()
+        result = result + recv_z[d].astype(jnp.float32)
+    gk_ref[...] = result[0]
+    gv_ref[...] = result[1]
 
     for d in range(1, n_high):
         line_copy(d).wait_send()
-        z_copies[d - 1].wait_send()
+    for d in range(n_high - 1):
+        z_copy(d).wait_send()
     for d in range(n_high):
         twin_copy(d, low).wait_send()
+        x_copy(d).wait_send()
     for d in range(1, n_ctx):
         remote(stats.at[ctx], stats.at[ctx], st_s.at[d], st_r.at[d],
                layer, lax.rem(ctx + d, n_ctx)).wait_send()
-    x_copy.wait_send()
 
     def sent_later(to, carry):
         remote(kv.at[ctx], kv.at[ctx], gc_s.at[to], gc_r.at[ctx], layer, to).wait_send()
@@ -269,7 +314,7 @@
     lax.fori_loop(ctx + 1, end, sent_later, 0)
 
     def sent_back(j, carry):
-        remote(send_ctx.at[j], recv_ctx.at[ctx], rc_s.at[j], rc_r.at[ctx], layer, j).wait_send()
+        remote(send_ctx.at[j], recv_ctx.at[ctx], rc_s.at[j], rc_r.at[ctx, 0], layer, j).wait_send()
         return carry
 
     lax.fori_loop(first, ctx, sent_back, 0)
@@ -294,19 +339,28 @@
             jax.ShapeDtypeStruct((rows, kv_width), f32),
             jax.ShapeDtypeStruct((classes, width), f32),
         ),
-        in_specs=[vmem] * 7,
+        in_specs=[pl.BlockSpec(memory_space=pltpu.HBM)] * 7,
         out_specs=(pl.BlockSpec(memory_space=pltpu.SMEM), vmem, vmem, vmem, vmem),
         scratch_shapes=[
+            pltpu.VMEM((local, width), bf),
+            pltpu.VMEM((classes, width), f32),
+            pltpu.VMEM((n_ctx, local), jnp.int32),
+            pltpu.VMEM((1, local), jnp.int32),
+            pltpu.VMEM((1, local), jnp.int32),
+            dma((7,)),
             pltpu.VMEM((n_ctx, n_layer, 2, rows, kv_width), bf),
             pltpu.VMEM((n_ctx, G, local, T), f32),
             pltpu.VMEM((classes, QUERY_HEADS, W, local), f32),
             pltpu.VMEM((G, 1, T), f32),
+            pltpu.VMEM((n_ctx, G, 1, T), f32),
             pltpu.VMEM((G, 1, T), f32),
             pltpu.VMEM((G, W, T), f32),
             pltpu.VMEM((G, W, T), bf),
             pltpu.VMEM((G, 1, T), f32),
             pltpu.VMEM((G, W, T), f32),
             pltpu.VMEM((n_layer, 2, rows, kv_width), f32),
+            pltpu.VMEM((2, rows, kv_width), f32),
+            pltpu.VMEM((STAT_ROWS, local), f32),
             pltpu.VMEM((n_ctx, STAT_ROWS, width), f32),
             pltpu.VMEM((n_ctx, n_layer, 2, rows, kv_width), bf),
             pltpu.VMEM((n_ctx, n_layer, 2, rows, kv_width), bf),
@@ -316,11 +370,11 @@
             pltpu.VMEM((n_high, 2, rows, kv_width), bf),
             dma((n_high,)), dma((n_high,)), dma((n_high,)), dma((n_high,)),
             dma((n_ctx,)), dma((n_ctx,)), dma((n_ctx,)), dma((n_ctx,)),
-            dma((n_ctx,)), dma((n_ctx,)), dma, dma,
+            dma((n_ctx,)), dma((n_ctx, n_high)), dma((n_high,)), dma((n_high,)),
             dma((n_high,)), dma((n_high,)),
         ],
         compiler_params=pltpu.CompilerParams(
-            collective_id=0, has_side_effects=True, vmem_limit_bytes=48 * 1024 * 1024),
+            collective_id=0, has_side_effects=True, vmem_limit_bytes=64 * 1024 * 1024 - 128 * 1024),
     )(
         queries[0], keys, values, jnp.swapaxes(head[0], 0, 1),
         segments.reshape(n_ctx, local), label_mask[None], labels[None],

time: 44.1 us -> 39.1 us (0.89)
  Pallas kernels: 34.7 us -> 32.2 us
  local copies, waits for them, and re-layouts: 6.51 us -> 4.17 us
    pallas_call x1, Pallas kernels: 34.7 us -> 32.2 us  [per_device(): pl.pallas_call(functools.partial(kernel, n_layer, n_ctx), out_shape=(jax....]
    unnamed x18 -> x10, local copies, waits for them, and re-layouts: 6.51 us -> 4.17 us
where the time goes in v2:
time: 39.1 us; the launch traced here: 38.8 us
  Pallas kernels  32.2 us (82%)
  local copies, waits for them, and re-layouts  4.17 us (11%)
  between operations  2.45 us (6%)
    pallas_call x1, Pallas kernels, per_device(): pl.pallas_call(functools.partial(kernel, n_layer, n_ctx), out_shape=(jax....  32.2 us
    unnamed x10, local copies, waits for them, and re-layouts  4.17 us

profile of v2, /device:TPU:1, one launch (start us, length us, event | category | flops | bytes accessed | tf_op | source)
XLA Modules:
  0.0 38.8 jit_solution(4476168436135417385)
XLA Ops:
  0.6 32.2 %shard_map.110 = (f32[1]{0:T(128)}, f32[128,1536]{1,0:T(8,128)}, f32[16,512]{1,0:T(8,128)}, f32[16,512]{1,0:T(8,128)}, f32[2,1536]{1,0:T(2,128)}) custom-call(bf16[128,1536]{1,0:T(8,128)(2,1)} %bitcast.12, bf16[16,512]{1,0:T(8,128)(2,1)} %k_in.1, bf16[16,512]{1,0:T(8,128)(2,1)} %v_in.1, f32[2,1536]{1,0:T(2,128)} %bitcast.13, s32[4,128]{1,0:T(4,128)} %bitcast.15, ...), custom_call_target="tpu_custom_call" | custom-call | tf_op jit(solution)/shard_map/pallas_call | solution.py:333
  33.5 0.0 copy-start.1
  33.5 2.1 %copy.18 = f32[1,128,1536]{2,1,0:T(8,128)} copy(f32[1,128,1536]{2,1,0:T(8,128)} %bitcast.11) | data formatting | bytes 1572864
  35.6 0.0 copy-done.1
  35.6 0.0 copy-start
  35.6 0.6 %copy.19 = f32[16,512]{1,0:T(8,128)} copy(f32[16,512]{1,0:T(8,128)S(1)} %copy-done.1) | data formatting | bytes 65536
  36.2 0.2 copy-done
  36.3 0.0 copy-start.2
  36.3 0.6 %copy.20 = f32[16,512]{1,0:T(8,128)} copy(f32[16,512]{1,0:T(8,128)S(1)} %copy-done) | data formatting | bytes 65536
  37.0 0.1 copy-done.2
  37.1 0.6 %copy.21 = f32[1,1536,2]{1,2,0:T(2,128)} copy(f32[1,1536,2]{1,2,0:T(2,128)S(1)} %bitcast.14) | data formatting | bytes 24576
Async XLA Ops:
  33.5 2.1 %copy-start.1 = (f32[16,512]{1,0:T(8,128)S(1)}, f32[16,512]{1,0:T(8,128)}, u32[]{:S(2)}) copy-start(f32[16,512]{1,0:T(8,128)} %get-tuple-element.22) | copy-start | bytes 98308
  35.6 0.8 %copy-start = (f32[16,512]{1,0:T(8,128)S(1)}, f32[16,512]{1,0:T(8,128)}, u32[]{:S(2)}) copy-start(f32[16,512]{1,0:T(8,128)} %get-tuple-element.23) | copy-start | bytes 98308
  36.3 0.7 %copy-start.2 = (f32[2,1536]{1,0:T(2,128)S(1)}, f32[2,1536]{1,0:T(2,128)}, u32[]{:S(2)}) copy-start(f32[2,1536]{1,0:T(2,128)} %get-tuple-element.14) | copy-start | bytes 36868

commit v3 on v2

--- a/solution.py
+++ b/solution.py
@@ -72,12 +72,6 @@
     for d in range(1, n_ctx):
         pl.semaphore_signal(
             barrier, inc=1, device_id=(layer, lax.rem(ctx + d, n_ctx)), device_id_type=MESH)
-    head_load.wait()
-    for k in range(classes):
-        for h in range(QUERY_HEADS):
-            row = head_ref[k : k + 1, h * W : (h + 1) * W]
-            hb[k, h] = jnp.transpose(jnp.broadcast_to(row, (local, W)))
-
     k_load.wait()
     v_load.wait()
     pl.semaphore_wait(barrier, n_high + n_ctx - 1)
@@ -134,8 +128,7 @@
     def score_block(i, carry):
         j = ctx - i
 
-        @pl.when(i > 0)
-        def _():
+        if not isinstance(i, int):
             remote(kv.at[j], kv.at[j], gc_s.at[j], gc_r.at[j], layer, ctx).wait_recv()
 
         seg_k = jnp.transpose(
@@ -145,9 +138,11 @@
         q_pos = ctx * local + lax.broadcasted_iota(jnp.int32, (local, local), 1)
         fill = jnp.where(same & (k_pos <= q_pos), 0.0, NEGATIVE_FILL)
         fill = jnp.concatenate([fill] * GROUP, axis=1)
+        ahead = dot(block_of(j, 0, 0), query_of(0), 1, 1)
         for g in range(KEY_VALUE_HEADS):
-            s = dot(block_of(j, 0, g), query_of(g), 1, 1) * (LOG2_E * W ** -0.5)
-            s = jnp.where(fill < 0.0, NEGATIVE_FILL, s)
+            s = jnp.where(fill < 0.0, NEGATIVE_FILL, ahead * (LOG2_E * W ** -0.5))
+            if g + 1 < KEY_VALUE_HEADS:
+                ahead = dot(block_of(j, 0, g + 1), query_of(g + 1), 1, 1)
             top = jnp.maximum(peak[g], jnp.max(s, axis=0, keepdims=True))
             fade = jnp.exp2(peak[g] - top)
             p = jnp.exp2(s - top)
@@ -158,7 +153,15 @@
             att[g] = att[g] * fade + dot(block_of(j, 1, g), p.astype(jnp.bfloat16), 0, 0)
         return carry
 
-    lax.fori_loop(0, count, score_block, 0)
+    score_block(0, 0)
+
+    head_load.wait()
+    for k in range(classes):
+        for h in range(QUERY_HEADS):
+            row = head_ref[k : k + 1, h * W : (h + 1) * W]
+            hb[k, h] = jnp.transpose(jnp.broadcast_to(row, (local, W)))
+
+    lax.fori_loop(1, count, score_block, 0)
 
     logits = [jnp.zeros((1, local), jnp.float32) for _ in range(classes)]
     parts = []
@@ -189,31 +192,36 @@
         rows_d[k : k + 1, :] = d_logits[k]
     rows_d[classes : classes + 1, :] = loss_rows
 
-    def back_block(i, carry):
-        j = first + i
+    def back_block(j, keep):
+        ahead = dot(block_of(j, 1, 0), datt[0], 1, 0)
         for g in range(KEY_VALUE_HEADS):
-            k_block, v_block = block_of(j, 0, g), block_of(j, 1, g)
-            da = datt[g]
-            dp = dot(v_block, da, 1, 0)
+            dp = ahead
+            if g + 1 < KEY_VALUE_HEADS:
+                ahead = dot(block_of(j, 1, g + 1), datt[g + 1], 1, 0)
             prob = score[j, g] * (total[g] * jnp.exp2(tops[j, g] - peak[g]))
             ds = (prob * ((dp - delta[g]) * W ** -0.5)).astype(jnp.bfloat16)
-            dqt[g] += dot(k_block, ds, 0, 0)
             cols = slice(g * W, (g + 1) * W)
-            grad[:, 0, :, cols] = dot(ds, query_of(g), 1, 0).reshape(n_layer, rows, W)
-            grad[:, 1, :, cols] = dot(prob.astype(jnp.bfloat16), da, 1, 1).reshape(
-                n_layer, rows, W)
-
-        @pl.when(j < ctx)
-        def _():
-            send_ctx[j] = grad[...].astype(jnp.bfloat16)
-            for d in range(n_high):
-                part = pl.ds(lax.rem(high + 1 + d, n_high) * 2, 2)
-                remote(send_ctx.at[j, part], recv_ctx.at[ctx, part], rc_s.at[j],
-                       rc_r.at[ctx, d], layer, j).start()
-
+            keep(1, cols, dot(prob.astype(jnp.bfloat16), datt[g], 1, 1))
+            keep(0, cols, dot(ds, query_of(g), 1, 0))
+            dqt[g] += dot(block_of(j, 0, g), ds, 0, 0)
+
+    def earlier_block(j, carry):
+        def keep(which, cols, value):
+            send_ctx[j, :, which, :, cols] = value.reshape(n_layer, rows, W).astype(jnp.bfloat16)
+
+        back_block(j, keep)
+        for d in range(n_high):
+            part = pl.ds(lax.rem(high + 1 + d, n_high) * 2, 2)
+            remote(send_ctx.at[j, part], recv_ctx.at[ctx, part], rc_s.at[j],
+                   rc_r.at[ctx, d], layer, j).start()
         return carry
 
-    lax.fori_loop(0, count, back_block, 0)
+    lax.fori_loop(first, ctx, earlier_block, 0)
+
+    def keep_own(which, cols, value):
+        grad[:, which, :, cols] = value.reshape(n_layer, rows, W)
+
+    back_block(ctx, keep_own)
 
     def side_work():
         stacked = jnp.concatenate(
@@ -320,6 +328,14 @@
     lax.fori_loop(first, ctx, sent_back, 0)
 
 
+def write_out(*refs):
+    copies = [pltpu.make_async_copy(refs[i], refs[4 + i], refs[8].at[i]) for i in range(4)]
+    for copy in copies:
+        copy.start()
+    for copy in copies:
+        copy.wait()
+
+
 def per_device(queries, keys, values, head, segments, label_mask, labels):
     n_layer, n_ctx = lax.axis_size("layer"), lax.axis_size("ctx")
     local, width = queries.shape[1:]
@@ -330,14 +346,13 @@
     vmem = pl.BlockSpec(memory_space=pltpu.VMEM)
     bf, f32 = jnp.bfloat16, jnp.float32
     dma = pltpu.SemaphoreType.DMA
-    loss, dq, gk, gv, hg = pl.pallas_call(
+    results = ((local, width), (rows, kv_width), (rows, kv_width), (classes, width))
+    results_bytes = 4 * sum(a * b for a, b in results)
+    loss, *computed = pl.pallas_call(
         functools.partial(kernel, n_layer, n_ctx),
         out_shape=(
             jax.ShapeDtypeStruct((1,), f32),
-            jax.ShapeDtypeStruct((local, width), f32),
-            jax.ShapeDtypeStruct((rows, kv_width), f32),
-            jax.ShapeDtypeStruct((rows, kv_width), f32),
-            jax.ShapeDtypeStruct((classes, width), f32),
+            *(pltpu.VMEM(shape, f32) for shape in results),
         ),
         in_specs=[pl.BlockSpec(memory_space=pltpu.HBM)] * 7,
         out_specs=(pl.BlockSpec(memory_space=pltpu.SMEM), vmem, vmem, vmem, vmem),
@@ -374,11 +389,19 @@
             dma((n_high,)), dma((n_high,)),
         ],
         compiler_params=pltpu.CompilerParams(
-            collective_id=0, has_side_effects=True, vmem_limit_bytes=64 * 1024 * 1024 - 128 * 1024),
+            collective_id=0, has_side_effects=True, vmem_limit_bytes=64 * 1024 * 1024 - results_bytes - 256 * 1024),
     )(
         queries[0], keys, values, jnp.swapaxes(head[0], 0, 1),
         segments.reshape(n_ctx, local), label_mask[None], labels[None],
     )
+    hbm = pl.BlockSpec(memory_space=pltpu.HBM)
+    dq, gk, gv, hg = pl.pallas_call(
+        write_out,
+        out_shape=tuple(jax.ShapeDtypeStruct(shape, f32) for shape in results),
+        in_specs=[vmem] * 4,
+        out_specs=(hbm,) * 4,
+        scratch_shapes=[dma((4,))],
+    )(*computed)
     return loss, dq[None], gk, gv, jnp.swapaxes(hg, 0, 1)[None]
 
 

time: 39.1 us -> 38.3 us (0.980)
  local copies, waits for them, and re-layouts: 4.17 us -> 2.69 us
  Pallas kernels: 32.2 us -> 33 us
    pallas_call x0 -> x1, Pallas kernels: none -> 2.08 us  [per_device(): pl.pallas_call(write_out, out_shape=tuple((jax.ShapeDtypeStruct(shape, f3...]
    unnamed x10 -> x8, local copies, waits for them, and re-layouts: 4.17 us -> 2.69 us
    pallas_call x1, Pallas kernels: 32.2 us -> 30.9 us  [per_device(): pl.pallas_call(functools.partial(kernel, n_layer, n_ctx), out_shape=(jax....]
where the time goes in v3:
time: 38.3 us; the launch traced here: 38.1 us
  Pallas kernels  33 us (86%)
  local copies, waits for them, and re-layouts  2.69 us (7%)
  between operations  2.42 us (6%)
    pallas_call x1, Pallas kernels, per_device(): pl.pallas_call(functools.partial(kernel, n_layer, n_ctx), out_shape=(jax....  30.9 us
    unnamed x8, local copies, waits for them, and re-layouts  2.69 us
    pallas_call x1, Pallas kernels, per_device(): pl.pallas_call(write_out, out_shape=tuple((jax.ShapeDtypeStruct(shape, f3...  2.08 us

profile of v3, /device:TPU:1, one launch (start us, length us, event | category | flops | bytes accessed | tf_op | source)
XLA Modules:
  0.0 38.1 jit_solution(10683530535851508866)
XLA Ops:
  0.6 30.9 %shard_map.110 = (f32[1]{0:T(128)}, f32[128,1536]{1,0:T(8,128)S(1)}, f32[16,512]{1,0:T(8,128)S(1)}, f32[16,512]{1,0:T(8,128)S(1)}, f32[2,1536]{1,0:T(2,128)S(1)}) custom-call(bf16[128,1536]{1,0:T(8,128)(2,1)} %bitcast.11, bf16[16,512]{1,0:T(8,128)(2,1)} %k_in.1, bf16[16,512]{1,0:T(8,128)(2,1)} %v_in.1, f32[2,1536]{1,0:T(2,128)} %bitcast.12, ...), custom_call_target="tpu_custom_call" | custom-call | tf_op jit(solution)/shard_map/pallas_call | solution.py:351
  31.5 0.0 copy-start
  31.6 0.9 %copy-done = f32[128,1536]{1,0:T(8,128)} copy-done((f32[128,1536]{1,0:T(8,128)}, f32[128,1536]{1,0:T(8,128)S(1)}, u32[]{:S(2)}) %copy-start) | copy-done | bytes 786456
  32.4 0.0 copy-start.1
  32.4 0.6 %copy-done.1 = f32[16,512]{1,0:T(8,128)} copy-done((f32[16,512]{1,0:T(8,128)}, f32[16,512]{1,0:T(8,128)S(1)}, u32[]{:S(2)}) %copy-start.1) | copy-done | bytes 32792
  33.0 0.0 copy-start.2
  33.0 0.6 %copy-done.2 = f32[16,512]{1,0:T(8,128)} copy-done((f32[16,512]{1,0:T(8,128)}, f32[16,512]{1,0:T(8,128)S(1)}, u32[]{:S(2)}) %copy-start.2) | copy-done | bytes 32792
  33.6 0.0 copy-start.3
  33.6 0.6 %copy-done.3 = f32[2,1536]{1,0:T(2,128)} copy-done((f32[2,1536]{1,0:T(2,128)}, f32[2,1536]{1,0:T(2,128)S(1)}, u32[]{:S(2)}) %copy-start.3) | copy-done | bytes 12312
  34.2 2.1 %shard_map.111 = (f32[128,1536]{1,0:T(8,128)}, f32[16,512]{1,0:T(8,128)}, f32[16,512]{1,0:T(8,128)}, f32[2,1536]{1,0:T(2,128)}) custom-call(f32[128,1536]{1,0:T(8,128)} %copy-done, f32[16,512]{1,0:T(8,128)} %copy-done.1, f32[16,512]{1,0:T(8,128)} %copy-done.2, f32[2,1536]{1,0:T(2,128)} %copy-done.3), custom_call_target="tpu_custom_call" | custom-call | tf_op jit(solution)/shard_map/pallas_call | solution.py:398
Async XLA Ops:
  31.5 0.9 %copy-start = (f32[128,1536]{1,0:T(8,128)}, f32[128,1536]{1,0:T(8,128)S(1)}, u32[]{:S(2)}) copy-start(f32[128,1536]{1,0:T(8,128)S(1)} %get-tuple-element.15.refs_0_) | copy-start | bytes 2359300
  32.4 0.6 %copy-start.1 = (f32[16,512]{1,0:T(8,128)}, f32[16,512]{1,0:T(8,128)S(1)}, u32[]{:S(2)}) copy-start(f32[16,512]{1,0:T(8,128)S(1)} %get-tuple-element.16.refs_1_) | copy-start | bytes 98308
  33.0 0.6 %copy-start.2 = (f32[16,512]{1,0:T(8,128)}, f32[16,512]{1,0:T(8,128)S(1)}, u32[]{:S(2)}) copy-start(f32[16,512]{1,0:T(8,128)S(1)} %get-tuple-element.17.refs_2_) | copy-start | bytes 98308
  33.6 0.6 %copy-start.3 = (f32[2,1536]{1,0:T(2,128)}, f32[2,1536]{1,0:T(2,128)S(1)}, u32[]{:S(2)}) copy-start(f32[2,1536]{1,0:T(2,128)S(1)} %get-tuple-element.18.refs_3_) | copy-start | bytes 36868

commit v4 on v3

--- a/solution.py
+++ b/solution.py
@@ -401,6 +401,7 @@
         in_specs=[vmem] * 4,
         out_specs=(hbm,) * 4,
         scratch_shapes=[dma((4,))],
+        compiler_params=pltpu.CompilerParams(vmem_limit_bytes=2 * results_bytes),
     )(*computed)
     return loss, dq[None], gk, gv, jnp.swapaxes(hg, 0, 1)[None]
 

time: 38.3 us -> 34.5 us (0.901)
  local copies, waits for them, and re-layouts: 2.69 us -> 0 us
  Pallas kernels: 33 us -> 31.8 us
    unnamed x8 -> x0, local copies, waits for them, and re-layouts: 2.69 us -> none
    pallas_call x1, Pallas kernels: 2.08 us -> 0.92 us  [per_device(): pl.pallas_call(write_out, out_shape=tuple((jax.ShapeDtypeStruct(shape, f3...]
where the time goes in v4:
time: 34.5 us; the launch traced here: 34.2 us
  Pallas kernels  31.8 us (92%)
  between operations  2.41 us (7%)
    pallas_call x1, Pallas kernels, per_device(): pl.pallas_call(functools.partial(kernel, n_layer, n_ctx), out_shape=(jax....  30.9 us
    pallas_call x1, Pallas kernels, per_device(): pl.pallas_call(write_out, out_shape=tuple((jax.ShapeDtypeStruct(shape, f3...  0.92 us

profile of v4, /device:TPU:1, one launch (start us, length us, event | category | flops | bytes accessed | tf_op | source)
XLA Modules:
  0.0 34.2 jit_solution(12935476842989321606)
XLA Ops:
  0.6 30.9 %shard_map.110 = (f32[1]{0:T(128)}, f32[128,1536]{1,0:T(8,128)S(1)}, f32[16,512]{1,0:T(8,128)S(1)}, f32[16,512]{1,0:T(8,128)S(1)}, f32[2,1536]{1,0:T(2,128)S(1)}) custom-call(bf16[128,1536]{1,0:T(8,128)(2,1)} %bitcast.11, bf16[16,512]{1,0:T(8,128)(2,1)} %k_in.1, bf16[16,512]{1,0:T(8,128)(2,1)} %v_in.1, f32[2,1536]{1,0:T(2,128)} %bitcast.12, ...), custom_call_target="tpu_custom_call" | custom-call | tf_op jit(solution)/shard_map/pallas_call | solution.py:351
  31.5 0.9 %shard_map.111 = (f32[128,1536]{1,0:T(8,128)}, f32[16,512]{1,0:T(8,128)}, f32[16,512]{1,0:T(8,128)}, f32[2,1536]{1,0:T(2,128)}) custom-call(f32[128,1536]{1,0:T(8,128)S(1)} %get-tuple-element.15.refs_0_, f32[16,512]{1,0:T(8,128)S(1)} %get-tuple-element.16.refs_1_, f32[16,512]{1,0:T(8,128)S(1)} %get-tuple-element.17.refs_2_, ...), custom_call_target="tpu_custom_call" | custom-call | tf_op jit(solution)/shard_map/pallas_call | solution.py:398

commit v5 on v4

--- a/solution.py
+++ b/solution.py
@@ -31,8 +31,9 @@
     loss_ref, dq_ref, gk_ref, gv_ref, hg_ref,
     q_ref, head_ref, seg_ref, mask_ref, label_ref, in_sem,
     kv, score, hb, peak, tops, total, att, datt, delta, dqt, grad, mine, rows_d, stats,
-    send_ctx, recv_ctx, send_x, recv_x, send_z, recv_z,
+    send_ctx, recv_ctx, send_x, recv_x, send_z, recv_z, recv_half, send_half, sum_half,
     gz_s, gz_r, gx_s, gx_r, gc_s, gc_r, st_s, st_r, rc_s, rc_r, rx_s, rx_r, rz_s, rz_r,
+    gl_s, gl_r, gf_s, gf_r, tw_s, tw_r, rh_s, rh_r,
 ):
     W = HEAD_WIDTH
     local = q_ref.shape[0]
@@ -47,6 +48,11 @@
     first = in_tail * tail
     end = tail + in_tail * (n_ctx - tail)
     count = ctx - first + 1
+    even = ((ctx % 2) == 0).astype(jnp.int32)
+    split = even * jnp.minimum(ctx + 2, end) + (1 - even) * end
+
+    def halved(j):
+        return ((j % 2) == 0) & (ctx - j >= 2)
 
     def remote(src, dst, s, r, to_layer, to_ctx):
         return pltpu.make_async_remote_copy(
@@ -76,12 +82,31 @@
     v_load.wait()
     pl.semaphore_wait(barrier, n_high + n_ctx - 1)
 
-    def to_later(piece):
-        def one(to, carry):
+    def to_later(piece, d=None):
+        def whole(to, carry):
             remote(kv.at[ctx, piece], kv.at[ctx, piece], gc_s.at[to], gc_r.at[ctx],
                    layer, to).start()
             return carry
-        lax.fori_loop(ctx + 1, end, one, 0)
+
+        def half(to, carry):
+            half_copy(to, d).start()
+            return carry
+
+        lax.fori_loop(ctx + 1, split, whole, 0)
+        if d is not None:
+            lax.fori_loop(split, end, half, 0)
+
+    def line_piece(d, side):
+        return lax.rem(high + n_high - d, n_high) * 2 + side
+
+    def half_copy(to, d):
+        piece = line_piece(d, low)
+        return remote(kv.at[ctx, piece], kv.at[ctx, piece], gl_s.at[to, d], gl_r.at[ctx, d],
+                      layer, to)
+
+    def forward_copy(j, d, side):
+        piece = line_piece(d, side)
+        return remote(kv.at[j, piece], kv.at[j, piece], gf_s.at[j, d], gf_r.at[j, d], twin, ctx)
 
     def line_copy(d):
         return remote(kv.at[ctx, layer], kv.at[ctx, layer], gz_s.at[d], gz_r.at[d],
@@ -94,14 +119,14 @@
     for d in range(1, n_high):
         line_copy(d).start()
     twin_copy(0, low).start()
-    to_later(layer)
+    to_later(layer, 0)
 
     for d in range(1, n_high):
         piece = lax.rem(high + n_high - d, n_high) * 2 + low
         remote(kv.at[ctx, piece], kv.at[ctx, piece], gz_s.at[d], gz_r.at[d],
                layer, ctx).wait_recv()
         twin_copy(d, low).start()
-        to_later(piece)
+        to_later(piece, d)
     for d in range(n_high):
         twin_copy(d, 1 - low).wait_recv()
         to_later(lax.rem(high + n_high - d, n_high) * 2 + (1 - low))
@@ -129,7 +154,14 @@
         j = ctx - i
 
         if not isinstance(i, int):
-            remote(kv.at[j], kv.at[j], gc_s.at[j], gc_r.at[j], layer, ctx).wait_recv()
+            @pl.when(halved(j))
+            def _():
+                for d in range(n_high):
+                    forward_copy(j, d, 1 - low).wait_recv()
+
+            @pl.when(jnp.logical_not(halved(j)))
+            def _():
+                remote(kv.at[j], kv.at[j], gc_s.at[j], gc_r.at[j], layer, ctx).wait_recv()
 
         seg_k = jnp.transpose(
             jnp.broadcast_to(seg_ref[pl.ds(j, 1), :], (local, local)).astype(jnp.float32))
@@ -155,6 +187,18 @@
 
     score_block(0, 0)
 
+    def pass_on(j, carry):
+        @pl.when(halved(j))
+        def _():
+            for d in range(n_high):
+                piece = line_piece(d, low)
+                remote(kv.at[j, piece], kv.at[j, piece], gl_s.at[j, d], gl_r.at[j, d],
+                       layer, ctx).wait_recv()
+                forward_copy(j, d, low).start()
+        return carry
+
+    lax.fori_loop(first, ctx, pass_on, 0)
+
     head_load.wait()
     for k in range(classes):
         for h in range(QUERY_HEADS):
@@ -205,23 +249,57 @@
             keep(0, cols, dot(ds, query_of(g), 1, 0))
             dqt[g] += dot(block_of(j, 0, g), ds, 0, 0)
 
-    def earlier_block(j, carry):
+    def place(d):
+        return lax.rem(high + 1 + d, n_high)
+
+    def twin_half(j, d):
+        return remote(send_ctx.at[j, place(d) * 2 + (1 - low)], recv_half.at[j, d],
+                      tw_s.at[j, d], tw_r.at[j, d], twin, ctx)
+
+    def half_sum(j, d):
+        return remote(send_half.at[j, d], sum_half.at[ctx, d], rh_s.at[j, d], rh_r.at[ctx, d],
+                      layer, j)
+
+    def earlier_block(i, carry):
+        j = ctx - 1 - i
+
         def keep(which, cols, value):
             send_ctx[j, :, which, :, cols] = value.reshape(n_layer, rows, W).astype(jnp.bfloat16)
 
         back_block(j, keep)
-        for d in range(n_high):
-            part = pl.ds(lax.rem(high + 1 + d, n_high) * 2, 2)
-            remote(send_ctx.at[j, part], recv_ctx.at[ctx, part], rc_s.at[j],
-                   rc_r.at[ctx, d], layer, j).start()
-        return carry
-
-    lax.fori_loop(first, ctx, earlier_block, 0)
+
+        @pl.when(halved(j))
+        def _():
+            for d in range(n_high):
+                twin_half(j, d).start()
+
+        @pl.when(jnp.logical_not(halved(j)))
+        def _():
+            for d in range(n_high):
+                part = pl.ds(place(d) * 2, 2)
+                remote(send_ctx.at[j, part], recv_ctx.at[ctx, part], rc_s.at[j],
+                       rc_r.at[ctx, d], layer, j).start()
+        return carry
+
+    lax.fori_loop(0, count - 1, earlier_block, 0)
 
     def keep_own(which, cols, value):
         grad[:, which, :, cols] = value.reshape(n_layer, rows, W)
 
     back_block(ctx, keep_own)
+
+    def add_halves(j, carry):
+        @pl.when(halved(j))
+        def _():
+            for d in range(n_high):
+                twin_half(j, d).wait_recv()
+                send_half[j, d] = (
+                    send_ctx[j, place(d) * 2 + low].astype(jnp.float32)
+                    + recv_half[j, d].astype(jnp.float32)).astype(jnp.bfloat16)
+                half_sum(j, d).start()
+        return carry
+
+    lax.fori_loop(first, ctx, add_halves, 0)
 
     def side_work():
         stacked = jnp.concatenate(
@@ -238,9 +316,6 @@
             g, r = h // GROUP, h % GROUP
             dq_ref[:, h * W : (h + 1) * W] = jnp.transpose(dqt[g, :, r * W : (r + 1) * W])
 
-    def place(d):
-        return lax.rem(high + 1 + d, n_high)
-
     def x_copy(d):
         return remote(send_x.at[d], recv_x.at[d], rx_s.at[d], rx_r.at[d], twin, ctx)
 
@@ -257,20 +332,31 @@
             grad[part] = grad[part] + recv_ctx[i, part].astype(jnp.float32)
             return carry
 
-        lax.fori_loop(ctx + 1, end, one, 0)
+        lax.fori_loop(ctx + 1, split, one, 0)
         send_x[d] = grad[place(d) * 2 + (1 - low)].astype(jnp.bfloat16)
         x_copy(d).start()
 
     def z_stage(d):
         x_copy(d).wait_recv()
-        value = grad[place(d) * 2 + low] + recv_x[d].astype(jnp.float32)
+        own = place(d) * 2 + low
+
+        def one(i, carry):
+            remote(send_half.at[i, d], sum_half.at[i, d], rh_s.at[i, d], rh_r.at[i, d],
+                   layer, ctx).wait_recv()
+            grad[own] = grad[own] + sum_half[i, d].astype(jnp.float32)
+            return carry
+
+        lax.fori_loop(split, end, one, 0)
+        value = grad[own] + recv_x[d].astype(jnp.float32)
         if d < n_high - 1:
             send_z[d] = value.astype(jnp.bfloat16)
             z_copy(d).start()
         else:
             mine[...] = value
 
-    @pl.when(ctx < end - 1)
+    waits = (ctx < end - 1) & (split == end)
+
+    @pl.when(waits)
     def _():
         side_work()
         for d in range(n_high):
@@ -279,7 +365,7 @@
                 z_stage(d - 1)
         z_stage(n_high - 1)
 
-    @pl.when(ctx == end - 1)
+    @pl.when(jnp.logical_not(waits))
     def _():
         for d in range(n_high):
             x_stage(d)
@@ -319,10 +405,27 @@
         remote(kv.at[ctx], kv.at[ctx], gc_s.at[to], gc_r.at[ctx], layer, to).wait_send()
         return carry
 
-    lax.fori_loop(ctx + 1, end, sent_later, 0)
+    lax.fori_loop(ctx + 1, split, sent_later, 0)
+
+    def sent_half(to, carry):
+        for d in range(n_high):
+            half_copy(to, d).wait_send()
+        return carry
+
+    lax.fori_loop(split, end, sent_half, 0)
 
     def sent_back(j, carry):
-        remote(send_ctx.at[j], recv_ctx.at[ctx], rc_s.at[j], rc_r.at[ctx, 0], layer, j).wait_send()
+        @pl.when(halved(j))
+        def _():
+            for d in range(n_high):
+                forward_copy(j, d, low).wait_send()
+                twin_half(j, d).wait_send()
+                half_sum(j, d).wait_send()
+
+        @pl.when(jnp.logical_not(halved(j)))
+        def _():
+            remote(send_ctx.at[j], recv_ctx.at[ctx], rc_s.at[j], rc_r.at[ctx, 0],
+                   layer, j).wait_send()
         return carry
 
     lax.fori_loop(first, ctx, sent_back, 0)
@@ -383,10 +486,12 @@
             pltpu.VMEM((n_high, 2, rows, kv_width), bf),
             pltpu.VMEM((n_high, 2, rows, kv_width), bf),
             pltpu.VMEM((n_high, 2, rows, kv_width), bf),
+            *[pltpu.VMEM((n_ctx, n_high, 2, rows, kv_width), bf)] * 3,
             dma((n_high,)), dma((n_high,)), dma((n_high,)), dma((n_high,)),
             dma((n_ctx,)), dma((n_ctx,)), dma((n_ctx,)), dma((n_ctx,)),
             dma((n_ctx,)), dma((n_ctx, n_high)), dma((n_high,)), dma((n_high,)),
             dma((n_high,)), dma((n_high,)),
+            *[dma((n_ctx, n_high))] * 8,
         ],
         compiler_params=pltpu.CompilerParams(
             collective_id=0, has_side_effects=True, vmem_limit_bytes=64 * 1024 * 1024 - results_bytes - 256 * 1024),

time: 34.5 us -> 37.1 us (1.075)
  the two profiles are of different devices: /device:TPU:1 before, /device:TPU:0 now
where the time goes in v5:
time: 37.1 us; the launch traced here: 36.9 us
  Pallas kernels  34.5 us (93%)
  between operations  2.41 us (6%)
    pallas_call x1, Pallas kernels, per_device(): pl.pallas_call(functools.partial(kernel, n_layer, n_ctx), out_shape=(jax....  33.5 us
    pallas_call x1, Pallas kernels, per_device(): pl.pallas_call(write_out, out_shape=tuple((jax.ShapeDtypeStruct(shape, f3...  0.92 us

profile of v5, /device:TPU:0, one launch (start us, length us, event | category | flops | bytes accessed | tf_op | source)
XLA Modules:
  0.0 36.9 jit_solution(8268272696901591066)
XLA Ops:
  0.6 33.5 %shard_map.110 = (f32[1]{0:T(128)}, f32[128,1536]{1,0:T(8,128)S(1)}, f32[16,512]{1,0:T(8,128)S(1)}, f32[16,512]{1,0:T(8,128)S(1)}, f32[2,1536]{1,0:T(2,128)S(1)}) custom-call(bf16[128,1536]{1,0:T(8,128)(2,1)} %bitcast.11, bf16[16,512]{1,0:T(8,128)(2,1)} %k_in.1, bf16[16,512]{1,0:T(8,128)(2,1)} %v_in.1, f32[2,1536]{1,0:T(2,128)} %bitcast.12, ...), custom_call_target="tpu_custom_call" | custom-call | tf_op jit(solution)/shard_map/pallas_call | solution.py:454
  34.2 0.9 %shard_map.111 = (f32[128,1536]{1,0:T(8,128)}, f32[16,512]{1,0:T(8,128)}, f32[16,512]{1,0:T(8,128)}, f32[2,1536]{1,0:T(2,128)}) custom-call(f32[128,1536]{1,0:T(8,128)S(1)} %get-tuple-element.15.refs_0_, f32[16,512]{1,0:T(8,128)S(1)} %get-tuple-element.16.refs_1_, f32[16,512]{1,0:T(8,128)S(1)} %get-tuple-element.17.refs_2_, ...), custom_call_target="tpu_custom_call" | custom-call | tf_op jit(solution)/shard_map/pallas_call | solution.py:503

commit v6 on v4

--- a/solution.py
+++ b/solution.py
@@ -32,7 +32,7 @@
     q_ref, head_ref, seg_ref, mask_ref, label_ref, in_sem,
     kv, score, hb, peak, tops, total, att, datt, delta, dqt, grad, mine, rows_d, stats,
     send_ctx, recv_ctx, send_x, recv_x, send_z, recv_z,
-    gz_s, gz_r, gx_s, gx_r, gc_s, gc_r, st_s, st_r, rc_s, rc_r, rx_s, rx_r, rz_s, rz_r,
+    gz_s, gz_r, gx_s, gx_r, gc_s, gc_r, st_s, st_r, rc_s, rc_r, rx_s, rx_r, rz_s, rz_r, rt_r,
 ):
     W = HEAD_WIDTH
     local = q_ref.shape[0]
@@ -70,16 +70,19 @@
             device_id_type=MESH)
     pl.semaphore_signal(barrier, inc=1, device_id=(twin, ctx), device_id_type=MESH)
     for d in range(1, n_ctx):
-        pl.semaphore_signal(
-            barrier, inc=1, device_id=(layer, lax.rem(ctx + d, n_ctx)), device_id_type=MESH)
+        for to_layer in (layer, twin):
+            pl.semaphore_signal(
+                barrier, inc=1, device_id=(to_layer, lax.rem(ctx + d, n_ctx)),
+                device_id_type=MESH)
     k_load.wait()
     v_load.wait()
-    pl.semaphore_wait(barrier, n_high + n_ctx - 1)
+    pl.semaphore_wait(barrier, n_high + 2 * (n_ctx - 1))
 
     def to_later(piece):
         def one(to, carry):
-            remote(kv.at[ctx, piece], kv.at[ctx, piece], gc_s.at[to], gc_r.at[ctx],
-                   layer, to).start()
+            for to_layer in (layer, twin):
+                remote(kv.at[ctx, piece], kv.at[ctx, piece], gc_s.at[to], gc_r.at[ctx],
+                       to_layer, to).start()
             return carry
         lax.fori_loop(ctx + 1, end, one, 0)
 
@@ -95,6 +98,12 @@
         line_copy(d).start()
     twin_copy(0, low).start()
     to_later(layer)
+
+    head_load.wait()
+    for k in range(classes):
+        for h in range(QUERY_HEADS):
+            row = head_ref[k : k + 1, h * W : (h + 1) * W]
+            hb[k, h] = jnp.transpose(jnp.broadcast_to(row, (local, W)))
 
     for d in range(1, n_high):
         piece = lax.rem(high + n_high - d, n_high) * 2 + low
@@ -104,7 +113,6 @@
         to_later(piece)
     for d in range(n_high):
         twin_copy(d, 1 - low).wait_recv()
-        to_later(lax.rem(high + n_high - d, n_high) * 2 + (1 - low))
 
     def block_of(j, which, g):
         part = kv[j, :, which, :, g * W : (g + 1) * W]
@@ -155,12 +163,6 @@
 
     score_block(0, 0)
 
-    head_load.wait()
-    for k in range(classes):
-        for h in range(QUERY_HEADS):
-            row = head_ref[k : k + 1, h * W : (h + 1) * W]
-            hb[k, h] = jnp.transpose(jnp.broadcast_to(row, (local, W)))
-
     lax.fori_loop(1, count, score_block, 0)
 
     logits = [jnp.zeros((1, local), jnp.float32) for _ in range(classes)]
@@ -205,15 +207,20 @@
             keep(0, cols, dot(ds, query_of(g), 1, 0))
             dqt[g] += dot(block_of(j, 0, g), ds, 0, 0)
 
+    def place(d):
+        return lax.rem(high + 1 + d, n_high)
+
     def earlier_block(j, carry):
         def keep(which, cols, value):
             send_ctx[j, :, which, :, cols] = value.reshape(n_layer, rows, W).astype(jnp.bfloat16)
 
         back_block(j, keep)
         for d in range(n_high):
-            part = pl.ds(lax.rem(high + 1 + d, n_high) * 2, 2)
-            remote(send_ctx.at[j, part], recv_ctx.at[ctx, part], rc_s.at[j],
+            pair = place(d) * 2
+            remote(send_ctx.at[j, pair + low], recv_ctx.at[ctx, pair + low], rc_s.at[j],
                    rc_r.at[ctx, d], layer, j).start()
+            remote(send_ctx.at[j, pair + (1 - low)], recv_ctx.at[ctx, pair + low], rc_s.at[j],
+                   rt_r.at[ctx, d], twin, j).start()
         return carry
 
     lax.fori_loop(first, ctx, earlier_block, 0)
@@ -238,9 +245,6 @@
             g, r = h // GROUP, h % GROUP
             dq_ref[:, h * W : (h + 1) * W] = jnp.transpose(dqt[g, :, r * W : (r + 1) * W])
 
-    def place(d):
-        return lax.rem(high + 1 + d, n_high)
-
     def x_copy(d):
         return remote(send_x.at[d], recv_x.at[d], rx_s.at[d], rx_r.at[d], twin, ctx)
 
@@ -249,43 +253,36 @@
                       place(d) * 2 + low, ctx)
 
     def x_stage(d):
-        part = pl.ds(place(d) * 2, 2)
-
-        def one(i, carry):
-            remote(send_ctx.at[i, part], recv_ctx.at[i, part], rc_s.at[i], rc_r.at[i, d],
-                   layer, ctx).wait_recv()
-            grad[part] = grad[part] + recv_ctx[i, part].astype(jnp.float32)
-            return carry
-
-        lax.fori_loop(ctx + 1, end, one, 0)
         send_x[d] = grad[place(d) * 2 + (1 - low)].astype(jnp.bfloat16)
         x_copy(d).start()
 
     def z_stage(d):
         x_copy(d).wait_recv()
-        value = grad[place(d) * 2 + low] + recv_x[d].astype(jnp.float32)
+        pair = place(d) * 2
+        own = pair + low
+        grad[own] = grad[own] + recv_x[d].astype(jnp.float32)
+
+        def one(i, carry):
+            for side, arrived in ((low, rc_r), (1 - low, rt_r)):
+                remote(send_ctx.at[i, pair + side], recv_ctx.at[i, pair + side], rc_s.at[i],
+                       arrived.at[i, d], layer, ctx).wait_recv()
+            grad[own] = grad[own] + (recv_ctx[i, own].astype(jnp.float32)
+                                     + recv_ctx[i, pair + (1 - low)].astype(jnp.float32))
+            return carry
+
+        lax.fori_loop(ctx + 1, end, one, 0)
+        value = grad[own]
         if d < n_high - 1:
             send_z[d] = value.astype(jnp.bfloat16)
             z_copy(d).start()
         else:
             mine[...] = value
 
-    @pl.when(ctx < end - 1)
-    def _():
-        side_work()
-        for d in range(n_high):
-            x_stage(d)
-            if d:
-                z_stage(d - 1)
-        z_stage(n_high - 1)
-
-    @pl.when(ctx == end - 1)
-    def _():
-        for d in range(n_high):
-            x_stage(d)
-        side_work()
-        for d in range(n_high):
-            z_stage(d)
+    for d in range(n_high):
+        x_stage(d)
+    side_work()
+    for d in range(n_high):
+        z_stage(d)
 
     for d in range(1, n_ctx):
         origin = lax.rem(ctx + n_ctx - d, n_ctx)
@@ -386,7 +383,7 @@
             dma((n_high,)), dma((n_high,)), dma((n_high,)), dma((n_high,)),
             dma((n_ctx,)), dma((n_ctx,)), dma((n_ctx,)), dma((n_ctx,)),
             dma((n_ctx,)), dma((n_ctx, n_high)), dma((n_high,)), dma((n_high,)),
-            dma((n_high,)), dma((n_high,)),
+            dma((n_high,)), dma((n_high,)), dma((n_ctx, n_high)),
         ],
         compiler_params=pltpu.CompilerParams(
             collective_id=0, has_side_effects=True, vmem_limit_bytes=64 * 1024 * 1024 - results_bytes - 256 * 1024),

time: 34.5 us -> 32.1 us (0.930)
  Pallas kernels: 31.8 us -> 29.5 us
    pallas_call x1, Pallas kernels: 30.9 us -> 28.5 us  [per_device(): pl.pallas_call(functools.partial(kernel, n_layer, n_ctx), out_shape=(jax....]
where the time goes in v6:
time: 32.1 us; the launch traced here: 31.9 us
  Pallas kernels  29.5 us (92%)
  between operations  2.41 us (8%)
    pallas_call x1, Pallas kernels, per_device(): pl.pallas_call(functools.partial(kernel, n_layer, n_ctx), out_shape=(jax....  28.5 us
    pallas_call x1, Pallas kernels, per_device(): pl.pallas_call(write_out, out_shape=tuple((jax.ShapeDtypeStruct(shape, f3...  0.92 us

profile of v6, /device:TPU:1, one launch (start us, length us, event | category | flops | bytes accessed | tf_op | source)
XLA Modules:
  0.0 31.9 jit_solution(14373651611986588742)
XLA Ops:
  0.6 28.5 %shard_map.110 = (f32[1]{0:T(128)}, f32[128,1536]{1,0:T(8,128)S(1)}, f32[16,512]{1,0:T(8,128)S(1)}, f32[16,512]{1,0:T(8,128)S(1)}, f32[2,1536]{1,0:T(2,128)S(1)}) custom-call(bf16[128,1536]{1,0:T(8,128)(2,1)} %bitcast.11, bf16[16,512]{1,0:T(8,128)(2,1)} %k_in.1, bf16[16,512]{1,0:T(8,128)(2,1)} %v_in.1, f32[2,1536]{1,0:T(2,128)} %bitcast.12, ...), custom_call_target="tpu_custom_call" | custom-call | tf_op jit(solution)/shard_map/pallas_call | solution.py:348
  29.2 0.9 %shard_map.111 = (f32[128,1536]{1,0:T(8,128)}, f32[16,512]{1,0:T(8,128)}, f32[16,512]{1,0:T(8,128)}, f32[2,1536]{1,0:T(2,128)}) custom-call(f32[128,1536]{1,0:T(8,128)S(1)} %get-tuple-element.15.refs_0_, f32[16,512]{1,0:T(8,128)S(1)} %get-tuple-element.16.refs_1_, f32[16,512]{1,0:T(8,128)S(1)} %get-tuple-element.17.refs_2_, ...), custom_call_target="tpu_custom_call" | custom-call | tf_op jit(solution)/shard_map/pallas_call | solution.py:395

commit v7 on v6

--- a/solution.py
+++ b/solution.py
@@ -30,7 +30,7 @@
     n_layer, n_ctx, q_in, k_in, v_in, head_in, seg_in, mask_in, label_in,
     loss_ref, dq_ref, gk_ref, gv_ref, hg_ref,
     q_ref, head_ref, seg_ref, mask_ref, label_ref, in_sem,
-    kv, score, hb, peak, tops, total, att, datt, delta, dqt, grad, mine, rows_d, stats,
+    kv, score, hb, peak, tops, total, att, datt, delta, dqt, scores16, grad, mine, rows_d, stats,
     send_ctx, recv_ctx, send_x, recv_x, send_z, recv_z,
     gz_s, gz_r, gx_s, gx_r, gc_s, gc_r, st_s, st_r, rc_s, rc_r, rx_s, rx_r, rz_s, rz_r, rt_r,
 ):
@@ -205,7 +205,7 @@
             cols = slice(g * W, (g + 1) * W)
             keep(1, cols, dot(prob.astype(jnp.bfloat16), datt[g], 1, 1))
             keep(0, cols, dot(ds, query_of(g), 1, 0))
-            dqt[g] += dot(block_of(j, 0, g), ds, 0, 0)
+            scores16[j, g] = ds
 
     def place(d):
         return lax.rem(high + 1 + d, n_high)
@@ -241,6 +241,14 @@
         for d in range(1, n_ctx):
             remote(stats.at[ctx], stats.at[ctx], st_s.at[d], st_r.at[d],
                    layer, lax.rem(ctx + d, n_ctx)).start()
+
+    def query_block(i, carry):
+        j = first + i
+        for g in range(KEY_VALUE_HEADS):
+            dqt[g] += dot(block_of(j, 0, g), scores16[j, g], 0, 0)
+        return carry
+
+    def query_out():
         for h in range(QUERY_HEADS):
             g, r = h // GROUP, h % GROUP
             dq_ref[:, h * W : (h + 1) * W] = jnp.transpose(dqt[g, :, r * W : (r + 1) * W])
@@ -280,9 +288,20 @@
 
     for d in range(n_high):
         x_stage(d)
+    lax.fori_loop(0, count, query_block, 0)
     side_work()
+
+    @pl.when(ctx < end - 1)
+    def _():
+        query_out()
+
     for d in range(n_high):
         z_stage(d)
+
+    @pl.when(ctx == end - 1)
+    def _():
+        query_out()
+
 
     for d in range(1, n_ctx):
         origin = lax.rem(ctx + n_ctx - d, n_ctx)
@@ -370,6 +389,7 @@
             pltpu.VMEM((G, W, T), bf),
             pltpu.VMEM((G, 1, T), f32),
             pltpu.VMEM((G, W, T), f32),
+            pltpu.VMEM((n_ctx, G, local, T), bf),
             pltpu.VMEM((n_layer, 2, rows, kv_width), f32),
             pltpu.VMEM((2, rows, kv_width), f32),
             pltpu.VMEM((STAT_ROWS, local), f32),

time: 32.1 us -> 32 us (level)
  no operation moved by 1% of the time
where the time goes in v7:
time: 32 us; the launch traced here: 31.8 us
  Pallas kernels  29.4 us (92%)
  between operations  2.41 us (8%)
    pallas_call x1, Pallas kernels, per_device(): pl.pallas_call(functools.partial(kernel, n_layer, n_ctx), out_shape=(jax....  28.4 us
    pallas_call x1, Pallas kernels, per_device(): pl.pallas_call(write_out, out_shape=tuple((jax.ShapeDtypeStruct(shape, f3...  0.92 us

profile of v7, /device:TPU:1, one launch (start us, length us, event | category | flops | bytes accessed | tf_op | source)
XLA Modules:
  0.0 31.8 jit_solution(10308647269606562507)
XLA Ops:
  0.6 28.4 %shard_map.110 = (f32[1]{0:T(128)}, f32[128,1536]{1,0:T(8,128)S(1)}, f32[16,512]{1,0:T(8,128)S(1)}, f32[16,512]{1,0:T(8,128)S(1)}, f32[2,1536]{1,0:T(2,128)S(1)}) custom-call(bf16[128,1536]{1,0:T(8,128)(2,1)} %bitcast.11, bf16[16,512]{1,0:T(8,128)(2,1)} %k_in.1, bf16[16,512]{1,0:T(8,128)(2,1)} %v_in.1, f32[2,1536]{1,0:T(2,128)} %bitcast.12, ...), custom_call_target="tpu_custom_call" | custom-call | tf_op jit(solution)/shard_map/pallas_call | solution.py:367
  29.1 0.9 %shard_map.111 = (f32[128,1536]{1,0:T(8,128)}, f32[16,512]{1,0:T(8,128)}, f32[16,512]{1,0:T(8,128)}, f32[2,1536]{1,0:T(2,128)}) custom-call(f32[128,1536]{1,0:T(8,128)S(1)} %get-tuple-element.15.refs_0_, f32[16,512]{1,0:T(8,128)S(1)} %get-tuple-element.16.refs_1_, f32[16,512]{1,0:T(8,128)S(1)} %get-tuple-element.17.refs_2_, ...), custom_call_target="tpu_custom_call" | custom-call | tf_op jit(solution)/shard_map/pallas_call | solution.py:415
